TPU v7x, 256 devices: a whole 4x4x8 slice. The times are simulated.
256 devices in a mesh: gx: 8 (over y, core), gy: 4 (over z_lo), grp: 8 (over x, z_hi).
Axes of the slice: x: 4, y: 4, z: 8 (z_hi: 2, z_lo: 4; z = z_hi * 4 + z_lo), core: 2. Of those that a mesh axis runs over, the one named last changes fastest.
Arguments:
- pressure: float32 [128, 64, 8192], P('gx', 'gy', 'grp'), may hold values from -6 to 6
- pressure_old: float32 [128, 64, 8192], P('gx', 'gy', 'grp'), may hold values from -6 to 6
- accumulation: float32 [128, 64, 8192], P('gx', 'gy', 'grp'), may hold values from 0.05 to 1
- permeability: float32 [3, 128, 64, 8192], P(None, 'gx', 'gy', 'grp'), may hold values from 0.05 to 20
- comp_block: int32 [8, 4, 8, 128], P('gx', 'gy', 'grp'), may hold values from 0 to 2047, as said below
- comp_owner: int32 [8, 4, 8, 128, 1], P('gx', 'gy', 'grp'), may hold values from 0 to 63; in each aligned block of 128 rows (0 to 127, 128 to 255, ..., all dimensions but the last counted through in order) at most 4 rows name the same one
- comp_well: int32 [8, 4, 8, 128], P('gx', 'gy', 'grp'), may hold values from 0 to 7
- comp_wi: float32 [8, 4, 8, 128, 128], P('gx', 'gy', 'grp'), may hold values from 0.5 to 4
- well_rate: float32 [8, 4, 8, 8], P('gx', 'gy', 'grp'), may hold values from -4096 to 4096
- well_storage: float32 [8, 4, 8, 8], P('gx', 'gy', 'grp'), may hold values from 256 to 4096
- well_bhp_old: float32 [8, 4, 8, 8], P('gx', 'gy', 'grp'), may hold values from -6 to 6
Outputs:
- pressure_new: float32 [128, 64, 8192], P('gx', 'gy', 'grp')
- well_bhp: float32 [8, 4, 8, 8], P('gx', 'gy', 'grp')
Inputs may be any that keep to these rules, and one draw needn't show every extreme that they name: `comp_block`: the 128 block numbers of one device are distinct. `comp_owner`: owner index o along gx and grp together (gx slowest), in the completion's own gy row; among the completions of one device at most 4 name one owner, a bound that some block reaches.
All inputs are finite; a program needn't handle non-finite values.
Results may differ from a plain program's by a relative error of at most 0.00022.
Values sent between devices are 32-bit elements; how exact they have to be, the bound alone decides.
A program may use at most 128 MiB of HBM per device.

v0:
```python
import jax
import jax.numpy as jnp
from jax import lax
from jax.sharding import PartitionSpec as P

CCX = 4
CCY = 4
CCZ = 8
SWEEPS = 4
COARSE_ITERS = 8


RELAXATION = 0.7


def padded_2(block, sides, width):
    for axis, dim in sides:
        count = lax.axis_size(axis)
        forward = [(i, i + 1) for i in range(count - 1)]
        backward = [(target, source) for source, target in forward]
        low = lax.ppermute(
            lax.slice_in_dim(block, block.shape[dim] - width, None, axis=dim), axis, forward
        )
        high = lax.ppermute(lax.slice_in_dim(block, 0, width, axis=dim), axis, backward)
        block = jnp.concatenate([low, block, high], axis=dim)
    return block


def harmonic(lower_k, upper_k):
    return 2.0 * lower_k * upper_k / (lower_k + upper_k)


def face_transmissibility(padded_perm):
    face_x = harmonic(padded_perm[0, :-1, 1:-1, 1:-1], padded_perm[0, 1:, 1:-1, 1:-1])
    face_y = harmonic(padded_perm[1, 1:-1, :-1, 1:-1], padded_perm[1, 1:-1, 1:, 1:-1])
    face_z = harmonic(padded_perm[2, 1:-1, 1:-1, :-1], padded_perm[2, 1:-1, 1:-1, 1:])
    return (face_x, face_y, face_z)


def neighbour_sum(padded, face_x, face_y, face_z):
    summed = face_x[1:] * padded[2:, 1:-1, 1:-1] + face_x[:-1] * padded[:-2, 1:-1, 1:-1]
    summed = (
        summed + face_y[:, 1:] * padded[1:-1, 2:, 1:-1] + face_y[:, :-1] * padded[1:-1, :-2, 1:-1]
    )
    summed = (
        summed
        + face_z[:, :, 1:] * padded[1:-1, 1:-1, 2:]
        + face_z[:, :, :-1] * padded[1:-1, 1:-1, :-2]
    )
    return summed


def face_total(face_x, face_y, face_z):
    return (
        face_x[1:]
        + face_x[:-1]
        + face_y[:, 1:]
        + face_y[:, :-1]
        + face_z[:, :, 1:]
        + face_z[:, :, :-1]
    )


def aggregate(values, agg_x, agg_y, agg_z):
    extent_x, extent_y, extent_z = values.shape
    shaped = values.reshape(
        extent_x // agg_x, agg_x, extent_y // agg_y, agg_y, extent_z // agg_z, agg_z
    )
    return shaped.sum(axis=(1, 3, 5))


def coarse_faces(face_x, face_y, face_z, agg_x, agg_y, agg_z):
    cells_x = (face_x.shape[0] - 1) // agg_x
    cells_y = (face_y.shape[1] - 1) // agg_y
    cells_z = (face_z.shape[2] - 1) // agg_z

    def plane_x(faces):
        return faces.reshape(cells_x, cells_y, agg_y, cells_z, agg_z).sum(axis=(2, 4))

    def plane_y(faces):
        return faces.reshape(cells_x, agg_x, cells_y, cells_z, agg_z).sum(axis=(1, 4))

    def plane_z(faces):
        return faces.reshape(cells_x, agg_x, cells_y, agg_y, cells_z).sum(axis=(1, 3))

    x_high = plane_x(face_x[agg_x::agg_x])
    x_low = plane_x(face_x[:-1:agg_x])
    y_high = plane_y(face_y[:, agg_y::agg_y])
    y_low = plane_y(face_y[:, :-1:agg_y])
    z_high = plane_z(face_z[:, :, agg_z::agg_z])
    z_low = plane_z(face_z[:, :, :-1:agg_z])
    return (x_high, x_low, y_high, y_low, z_high, z_low)


def coarse_sweep(current, padded, coarse_rhs, coarse_diag, faces):
    x_high, x_low, y_high, y_low, z_high, z_low = faces
    summed = x_high * padded[2:, 1:-1, 1:-1] + x_low * padded[:-2, 1:-1, 1:-1]
    summed = summed + y_high * padded[1:-1, 2:, 1:-1] + y_low * padded[1:-1, :-2, 1:-1]
    summed = summed + z_high * padded[1:-1, 1:-1, 2:] + z_low * padded[1:-1, 1:-1, :-2]
    return current + RELAXATION * (coarse_rhs - (coarse_diag * current - summed)) / coarse_diag


def per_device(
    pressure,
    pressure_old,
    accumulation,
    permeability,
    comp_block,
    comp_owner,
    comp_well,
    comp_wi,
    well_rate,
    well_storage,
    well_bhp_old,
):
    size_x, size_y, size_z = pressure.shape
    stacked = jnp.concatenate([pressure[None], permeability], axis=0)
    padded = padded_2(stacked, (("gx", 1), ("gy", 2), ("grp", 3)), 1)
    face_x, face_y, face_z = face_transmissibility(padded[1:])
    padded_pressure = padded[0]
    summed_faces = face_total(face_x, face_y, face_z)
    blocks = comp_block.reshape(-1)
    owners = comp_owner.reshape(-1)
    labels = comp_well.reshape(-1).astype(jnp.float32)
    weights = comp_wi.reshape(-1, 128)
    completions = blocks.shape[0]
    senders = lax.axis_size("gx") * lax.axis_size("grp")
    capacity = 2 * completions // senders
    well_count = well_rate.shape[-1]
    storage = well_storage.reshape(-1)
    previous = well_bhp_old.reshape(-1)
    targets = well_rate.reshape(-1)
    matches = (owners[:, None] == jnp.arange(senders, dtype=jnp.int32)[None, :]).astype(jnp.int32)
    position = jnp.sum(jnp.cumsum(matches, axis=0) * matches, axis=1) - 1
    target_slot = owners * capacity + position
    pressure_rows = pressure.reshape(-1, 128)[blocks]
    payload = (
        jnp.zeros((senders * capacity, 256), jnp.float32)
        .at[target_slot]
        .set(jnp.concatenate([pressure_rows, weights], axis=1))
    )
    tags = jnp.zeros((senders * capacity,), jnp.float32).at[target_slot].set(labels)
    arrived, arrived_tags = (
        lax.all_to_all(
            payload.reshape(senders, capacity, 256),
            ("gx", "grp"),
            split_axis=0,
            concat_axis=0,
            tiled=True,
        ),
        lax.all_to_all(
            tags.reshape(senders, capacity), ("gx", "grp"), split_axis=0, concat_axis=0, tiled=True
        ),
    )
    arrived = arrived.reshape(-1, 256)
    belong = (
        arrived_tags.reshape(-1)[:, None] == jnp.arange(well_count, dtype=jnp.float32)[None, :]
    ).astype(jnp.float32)
    weighted = jnp.sum(arrived[:, 128:] * arrived[:, :128], axis=1)
    total_wi = jnp.sum(arrived[:, 128:], axis=1)
    numerator = jnp.dot(weighted, belong, precision=lax.Precision.HIGHEST)
    denominator = jnp.dot(total_wi, belong, precision=lax.Precision.HIGHEST)
    bottom_hole = (numerator + storage * previous - targets) / (denominator + storage)
    slot_pressure = jnp.dot(belong, bottom_hole, precision=lax.Precision.HIGHEST)
    returned = arrived[:, 128:] * (arrived[:, :128] - slot_pressure[:, None])
    answer = lax.all_to_all(
        returned.reshape(senders, capacity, 128),
        ("gx", "grp"),
        split_axis=0,
        concat_axis=0,
        tiled=True,
    )
    well_terms = answer.reshape(-1, 128)[target_slot]
    empty = jnp.zeros((size_x * size_y * size_z // 128, 128), jnp.float32)
    q_grid = empty.at[blocks].add(well_terms).reshape(size_x, size_y, size_z)
    w_grid = empty.at[blocks].add(weights).reshape(size_x, size_y, size_z)
    resid = (
        accumulation * (pressure - pressure_old)
        + summed_faces * pressure
        - neighbour_sum(padded_pressure, face_x, face_y, face_z)
        + q_grid
    )
    diagonal = accumulation + w_grid + summed_faces
    agg_x, agg_y, agg_z = (size_x // CCX, size_y // CCY, size_z // CCZ)
    coarse_rhs = aggregate(-resid, agg_x, agg_y, agg_z)
    x_high, x_low, y_high, y_low, z_high, z_low = coarse_faces(
        face_x, face_y, face_z, agg_x, agg_y, agg_z
    )
    coarse_diag = (
        aggregate(accumulation + w_grid, agg_x, agg_y, agg_z)
        + x_high
        + x_low
        + y_high
        + y_low
        + z_high
        + z_low
    )
    local_faces = (x_high, x_low, y_high, y_low, z_high, z_low)
    current = jnp.zeros_like(coarse_rhs)
    for step_index in range(COARSE_ITERS):
        bordered = padded_2(current, (("gy", 1), ("grp", 2)), 1)
        bordered = jnp.pad(bordered, ((1, 1), (0, 0), (0, 0)))
        current = coarse_sweep(current, bordered, coarse_rhs, coarse_diag, local_faces)
    delta = jnp.broadcast_to(
        current[:, None, :, None, :, None], (CCX, agg_x, CCY, agg_y, CCZ, agg_z)
    ).reshape(size_x, size_y, size_z)
    for sweep_index in range(SWEEPS):
        bordered_delta = padded_2(delta, (("gx", 0), ("gy", 1), ("grp", 2)), 1)
        applied = diagonal * delta - neighbour_sum(bordered_delta, face_x, face_y, face_z)
        delta = delta + RELAXATION * (-resid - applied) / diagonal
    return (pressure + delta, bottom_hole.reshape(1, 1, 1, well_count))


def solution(mesh):
    return jax.shard_map(
        per_device,
        mesh=mesh,
        in_specs=(
            P("gx", "gy", "grp"),
            P("gx", "gy", "grp"),
            P("gx", "gy", "grp"),
            P(None, "gx", "gy", "grp"),
            P("gx", "gy", "grp", None),
            P("gx", "gy", "grp", None, None),
            P("gx", "gy", "grp", None),
            P("gx", "gy", "grp", None, None),
            P("gx", "gy", "grp", None),
            P("gx", "gy", "grp", None),
            P("gx", "gy", "grp", None),
        ),
        out_specs=(P("gx", "gy", "grp"), P("gx", "gy", "grp", None)),
        check_vma=False,
    )
```

profile of v0, /device:TPU:46, one launch (start us, length us, event | category | flops | bytes accessed | tf_op | source)
XLA Modules:
  0.0 525.6 jit_solution(2801969153016926091)
XLA Ops:
  16.2 13.6 %all-to-all-start.1 = ((f32[64,1,4]{2,1,0:T(1,128)}), f32[64,1,4]{2,1,0:T(1,128)S(1)}, u32[]{:S(2)}, u32[]{:S(2)}) async-start(f32[64,1,4]{2,1,0:T(1,128)} %bitcast.16), calls=%async_computation.1 | async-start | bytes 65536 | tf_op jit(solution)/shard_map/all_to_all | solution.py:151
  37.3 7.3 %collective-permute-start.8 = (f32[4,6,1]{2,1,0:T(8,128)S(1)}, f32[4,6,1]{2,1,0:T(8,128)S(1)}, u32[]{:S(2)}, u32[]{:S(2)}) collective-permute-start(f32[4,6,1]{2,1,0:T(8,128)S(1)} %get-tuple-element.55), channel_id=1, source_target_pairs={{0,1},{1,2},{2,3},{3,4},{4,5},{5,6},{6,7},{8,9},{9,10},{10,11},{11... | collective-permute-start | bytes 296 | tf_op jit(solution)/shard_map/ppermute | solution.py:21
  55.0 9.4 %all-to-all-start = ((f32[64,4,256]{2,1,0:T(4,128)}), f32[64,4,256]{2,1,0:T(4,128)}, u32[]{:S(2)}, u32[]{:S(2)}) async-start(f32[64,4,256]{2,1,0:T(4,128)} %reshape.146), calls=%async_computation | async-start | bytes 524288 | tf_op jit(solution)/shard_map/all_to_all | solution.py:144
  86.1 12.9 %all-to-all-start.2 = ((f32[64,4,128]{2,1,0:T(4,128)}), f32[64,4,128]{2,1,0:T(4,128)}, u32[]{:S(2)}, u32[]{:S(2)}) async-start(f32[64,4,128]{2,1,0:T(4,128)} %bitcast.26), calls=%async_computation.2 | async-start | bytes 262144 | tf_op jit(solution)/shard_map/all_to_all | solution.py:166
  108.4 7.3 %collective-permute-start.4 = (f32[4,18,18,1]{2,0,3,1:T(4,128)S(1)}, f32[4,18,18,1]{2,0,3,1:T(4,128)S(1)}, u32[]{:S(2)}, u32[]{:S(2)}) collective-permute-start(f32[4,18,18,1]{2,0,3,1:T(4,128)S(1)} %copy.54), channel_id=1, source_target_pairs={{0,1},{1,2},{2,3},{3,4},{4,5},{5,6},{6,7},{8,9},{9,10},{10,11},{11... | collective-permute-start | bytes 15560 | tf_op jit(solution)/shard_map/ppermute | solution.py:21
  131.1 10.8 %concatenate.286 = f32[4,18,18,1026]{3,2,1,0:T(8,128)} concatenate(f32[4,18,18,1]{3,2,1,0:T(8,128)S(1)} %copy.55, f32[4,18,18,1024]{3,2,1,0:T(8,128)} %copy-done.7, f32[4,18,18,1]{3,2,1,0:T(8,128)} %copy.57), dimensions={3} | concatenate | bytes 10637568 | tf_op jit(solution)/shard_map/concatenate | solution.py:25
  155.0 8.3 %fusion.222 = (f32[16,16,1024]{2,1,0:T(8,128)}, f32[16,16,1024]{2,1,0:T(8,128)S(1)}) fusion(f32[16,16,1024]{2,1,0:T(8,128)} %param.13, f32[16,16,1024]{2,1,0:T(8,128)} %reshape.155, f32[16,16,1024]{2,1,0:T(8,128)} %reshape.153, f32[18,18,1026]{2,1,0:T(8,128)} %slice_bitcast_fusion, f32[16,16,1024]{2,1,0:T(8,128)S(1)} %copy-done.3, ...), kind=kLoop, calls=%fused_computation.504 | loop fusion | flops 6291456 | bytes 19922944 | tf_op jit(solution)/shard_map/add | solution.py:190
  179.3 6.4 %collective-permute-start.12 = (f32[4,6,1]{2,1,0:T(8,128)S(1)}, f32[4,6,1]{2,1,0:T(8,128)S(1)}, u32[]{:S(2)}, u32[]{:S(2)}) collective-permute-start(f32[4,6,1]{2,1,0:T(8,128)S(1)} %get-tuple-element.53), channel_id=1, source_target_pairs={{0,1},{1,2},{2,3},{3,4},{4,5},{5,6},{6,7},{8,9},{9,10},{10,11},{11... | collective-permute-start | bytes 296 | tf_op jit(solution)/shard_map/ppermute | solution.py:21
  205.9 8.7 %collective-permute-start.17 = (f32[4,6,1]{2,1,0:T(8,128)S(1)}, f32[4,6,1]{2,1,0:T(8,128)S(1)}, u32[]{:S(2)}, u32[]{:S(2)}) collective-permute-start(f32[4,6,1]{2,1,0:T(8,128)S(1)} %get-tuple-element.50), channel_id=1, source_target_pairs={{1,0},{2,1},{3,2},{4,3},{5,4},{6,5},{7,6},{9,8},{10,9},{11,10},{12... | collective-permute-start | bytes 296 | tf_op jit(solution)/shard_map/ppermute | solution.py:24
  225.7 9.0 %collective-permute-start.21 = (f32[4,6,1]{2,1,0:T(8,128)S(1)}, f32[4,6,1]{2,1,0:T(8,128)S(1)}, u32[]{:S(2)}, u32[]{:S(2)}) collective-permute-start(f32[4,6,1]{2,1,0:T(8,128)S(1)} %get-tuple-element.48), channel_id=1, source_target_pairs={{1,0},{2,1},{3,2},{4,3},{5,4},{6,5},{7,6},{9,8},{10,9},{11,10},{12... | collective-permute-start | bytes 296 | tf_op jit(solution)/shard_map/ppermute | solution.py:24
  245.7 9.0 %collective-permute-start.25 = (f32[4,6,1]{2,1,0:T(8,128)S(1)}, f32[4,6,1]{2,1,0:T(8,128)S(1)}, u32[]{:S(2)}, u32[]{:S(2)}) collective-permute-start(f32[4,6,1]{2,1,0:T(8,128)S(1)} %get-tuple-element.46), channel_id=1, source_target_pairs={{1,0},{2,1},{3,2},{4,3},{5,4},{6,5},{7,6},{9,8},{10,9},{11,10},{12... | collective-permute-start | bytes 296 | tf_op jit(solution)/shard_map/ppermute | solution.py:24
  265.8 9.0 %collective-permute-start.29 = (f32[4,6,1]{2,1,0:T(8,128)S(1)}, f32[4,6,1]{2,1,0:T(8,128)S(1)}, u32[]{:S(2)}, u32[]{:S(2)}) collective-permute-start(f32[4,6,1]{2,1,0:T(8,128)S(1)} %get-tuple-element.44), channel_id=1, source_target_pairs={{1,0},{2,1},{3,2},{4,3},{5,4},{6,5},{7,6},{9,8},{10,9},{11,10},{12... | collective-permute-start | bytes 296 | tf_op jit(solution)/shard_map/ppermute | solution.py:24
  285.9 9.0 %collective-permute-start.33 = (f32[4,6,1]{2,1,0:T(8,128)S(1)}, f32[4,6,1]{2,1,0:T(8,128)S(1)}, u32[]{:S(2)}, u32[]{:S(2)}) collective-permute-start(f32[4,6,1]{2,1,0:T(8,128)S(1)} %get-tuple-element.42), channel_id=1, source_target_pairs={{1,0},{2,1},{3,2},{4,3},{5,4},{6,5},{7,6},{9,8},{10,9},{11,10},{12... | collective-permute-start | bytes 296 | tf_op jit(solution)/shard_map/ppermute | solution.py:24
  306.0 9.1 %collective-permute-start.37 = (f32[4,6,1]{2,1,0:T(8,128)S(1)}, f32[4,6,1]{2,1,0:T(8,128)S(1)}, u32[]{:S(2)}, u32[]{:S(2)}) collective-permute-start(f32[4,6,1]{2,1,0:T(8,128)S(1)} %get-tuple-element.40), channel_id=1, source_target_pairs={{1,0},{2,1},{3,2},{4,3},{5,4},{6,5},{7,6},{9,8},{10,9},{11,10},{12... | collective-permute-start | bytes 296 | tf_op jit(solution)/shard_map/ppermute | solution.py:24
  340.1 9.0 %collective-permute-start.42 = (f32[18,18,1]{2,1,0:T(8,128)S(1)}, f32[18,18,1]{2,1,0:T(8,128)S(1)}, u32[]{:S(2)}, u32[]{:S(2)}) collective-permute-start(f32[18,18,1]{2,1,0:T(8,128)S(1)} %get-tuple-element.18), channel_id=1, source_target_pairs={{1,0},{2,1},{3,2},{4,3},{5,4},{6,5},{7,6},{9,8},{10,9},{11,10},{12... | collective-permute-start | bytes 3896 | tf_op jit(solution)/shard_map/ppermute | solution.py:24
  357.4 15.7 %collective-permute-done.43 = f32[18,18,1]{2,1,0:T(8,128)S(1)} collective-permute-done((f32[18,18,1]{2,1,0:T(8,128)S(1)}, f32[18,18,1]{2,1,0:T(8,128)S(1)}, u32[]{:S(2)}, u32[]{:S(2)}) %collective-permute-start.43) | collective-permute-done | bytes 1328 | tf_op jit(solution)/shard_map/ppermute | solution.py:21
  393.2 9.0 %collective-permute-start.48 = (f32[18,18,1]{2,1,0:T(8,128)S(1)}, f32[18,18,1]{2,1,0:T(8,128)S(1)}, u32[]{:S(2)}, u32[]{:S(2)}) collective-permute-start(f32[18,18,1]{2,1,0:T(8,128)S(1)} %get-tuple-element.16), channel_id=1, source_target_pairs={{1,0},{2,1},{3,2},{4,3},{5,4},{6,5},{7,6},{9,8},{10,9},{11,10},{12... | collective-permute-start | bytes 3896 | tf_op jit(solution)/shard_map/ppermute | solution.py:24
  404.1 10.9 %collective-permute-done.48 = f32[18,18,1]{2,1,0:T(8,128)S(1)} collective-permute-done((f32[18,18,1]{2,1,0:T(8,128)S(1)}, f32[18,18,1]{2,1,0:T(8,128)S(1)}, u32[]{:S(2)}, u32[]{:S(2)}) %collective-permute-start.48) | collective-permute-done | bytes 1328 | tf_op jit(solution)/shard_map/ppermute | solution.py:24
  415.1 9.7 %collective-permute-done.49 = f32[18,18,1]{2,1,0:T(8,128)S(1)} collective-permute-done((f32[18,18,1]{2,1,0:T(8,128)S(1)}, f32[18,18,1]{2,1,0:T(8,128)S(1)}, u32[]{:S(2)}, u32[]{:S(2)}) %collective-permute-start.49) | collective-permute-done | bytes 1328 | tf_op jit(solution)/shard_map/ppermute | solution.py:21
  445.4 8.6 %collective-permute-start.54 = (f32[18,18,1]{2,1,0:T(8,128)S(1)}, f32[18,18,1]{2,1,0:T(8,128)S(1)}, u32[]{:S(2)}, u32[]{:S(2)}) collective-permute-start(f32[18,18,1]{2,1,0:T(8,128)S(1)} %get-tuple-element.14), channel_id=1, source_target_pairs={{1,0},{2,1},{3,2},{4,3},{5,4},{6,5},{7,6},{9,8},{10,9},{11,10},{12... | collective-permute-start | bytes 3896 | tf_op jit(solution)/shard_map/ppermute | solution.py:24
  455.9 11.1 %collective-permute-done.54 = f32[18,18,1]{2,1,0:T(8,128)S(1)} collective-permute-done((f32[18,18,1]{2,1,0:T(8,128)S(1)}, f32[18,18,1]{2,1,0:T(8,128)S(1)}, u32[]{:S(2)}, u32[]{:S(2)}) %collective-permute-start.54) | collective-permute-done | bytes 1328 | tf_op jit(solution)/shard_map/ppermute | solution.py:24
  467.0 9.7 %collective-permute-done.55 = f32[18,18,1]{2,1,0:T(8,128)S(1)} collective-permute-done((f32[18,18,1]{2,1,0:T(8,128)S(1)}, f32[18,18,1]{2,1,0:T(8,128)S(1)}, u32[]{:S(2)}, u32[]{:S(2)}) %collective-permute-start.55) | collective-permute-done | bytes 1328 | tf_op jit(solution)/shard_map/ppermute | solution.py:21
  499.7 7.3 %collective-permute-start.61 = (f32[18,18,1]{2,1,0:T(8,128)S(1)}, f32[18,18,1]{2,1,0:T(8,128)S(1)}, u32[]{:S(2)}, u32[]{:S(2)}) collective-permute-start(f32[18,18,1]{2,1,0:T(8,128)S(1)} %get-tuple-element.13), channel_id=1, source_target_pairs={{0,1},{1,2},{2,3},{3,4},{4,5},{5,6},{6,7},{8,9},{9,10},{10,11},{11... | collective-permute-start | bytes 3896 | tf_op jit(solution)/shard_map/ppermute | solution.py:21
  510.3 10.3 %collective-permute-done.61 = f32[18,18,1]{2,1,0:T(8,128)S(1)} collective-permute-done((f32[18,18,1]{2,1,0:T(8,128)S(1)}, f32[18,18,1]{2,1,0:T(8,128)S(1)}, u32[]{:S(2)}, u32[]{:S(2)}) %collective-permute-start.61) | collective-permute-done | bytes 1328 | tf_op jit(solution)/shard_map/ppermute | solution.py:21
  (306 shorter events, 292.0 us)
Async XLA Ops:
  0.6 36.5 %collective-permute-start.6 = (f32[4,1,8]{2,1,0:T(1,128)S(1)}, f32[4,1,8]{2,1,0:T(1,128)S(1)}, u32[]{:S(2)}, u32[]{:S(2)}) collective-permute-start(f32[4,1,8]{2,1,0:T(1,128)S(1)} %broadcast.97), channel_id=1, source_target_pairs={{0,8},{8,16},{16,24},{1,9},{9,17},{17,25},{2,10},{10,18},{18,26},{... | collective-permute-start | bytes 392 | tf_op jit(solution)/shard_map/ppermute | solution.py:21
  4.5 32.7 %collective-permute-start.7 = (f32[4,1,8]{2,1,0:T(1,128)S(1)}, f32[4,1,8]{2,1,0:T(1,128)S(1)}, u32[]{:S(2)}, u32[]{:S(2)}) collective-permute-start(f32[4,1,8]{2,1,0:T(1,128)S(1)} %broadcast.97), channel_id=1, source_target_pairs={{8,0},{16,8},{24,16},{9,1},{17,9},{25,17},{10,2},{18,10},{26,18},{... | collective-permute-start | bytes 392 | tf_op jit(solution)/shard_map/ppermute | solution.py:24
  8.5 57.3 %collective-permute-start = (f32[4,1,16,1024]{3,2,1,0:T(8,128)}, f32[4,1,16,1024]{3,2,1,0:T(8,128)S(1)}, u32[]{:S(2)}, u32[]{:S(2)}) collective-permute-start(f32[4,1,16,1024]{3,2,1,0:T(8,128)} %get-tuple-element.10), channel_id=1, source_target_pairs={{0,32},{32,64},{64,96},{96,128},{128,160},{160,192},{192,224},{1,3... | collective-permute-start | bytes 786440 | tf_op jit(solution)/shard_map/ppermute | solution.py:21
  10.4 55.4 %collective-permute-start.1 = (f32[4,1,16,1024]{3,2,1,0:T(8,128)S(1)}, f32[4,1,16,1024]{3,2,1,0:T(8,128)S(1)}, u32[]{:S(2)}, u32[]{:S(2)}) collective-permute-start(f32[4,1,16,1024]{3,2,1,0:T(8,128)S(1)} %get-tuple-element.11), channel_id=1, source_target_pairs={{32,0},{64,32},{96,64},{128,96},{160,128},{192,160},{224,192},{33,... | collective-permute-start | bytes 786440 | tf_op jit(solution)/shard_map/ppermute | solution.py:24
  16.2 38.7 %all-to-all-start.1 = ((f32[64,1,4]{2,1,0:T(1,128)}), f32[64,1,4]{2,1,0:T(1,128)S(1)}, u32[]{:S(2)}, u32[]{:S(2)}) async-start(f32[64,1,4]{2,1,0:T(1,128)} %bitcast.16), calls=%async_computation.1 | async-start | bytes 65536 | tf_op jit(solution)/shard_map/all_to_all | solution.py:151
  55.0 25.8 %all-to-all-start = ((f32[64,4,256]{2,1,0:T(4,128)}), f32[64,4,256]{2,1,0:T(4,128)}, u32[]{:S(2)}, u32[]{:S(2)}) async-start(f32[64,4,256]{2,1,0:T(4,128)} %reshape.146), calls=%async_computation | async-start | bytes 524288 | tf_op jit(solution)/shard_map/all_to_all | solution.py:144
  69.4 29.6 %collective-permute-start.2 = (f32[4,18,1,1024]{3,2,1,0:T(1,128)}, f32[4,18,1,1024]{3,2,1,0:T(1,128)S(1)}, u32[]{:S(2)}, u32[]{:S(2)}) collective-permute-start(f32[4,18,1,1024]{3,2,1,0:T(1,128)} %get-tuple-element.8), channel_id=1, source_target_pairs={{0,8},{8,16},{16,24},{1,9},{9,17},{17,25},{2,10},{10,18},{18,26},{... | collective-permute-start | bytes 884744 | tf_op jit(solution)/shard_map/ppermute | solution.py:21
  72.3 26.7 %collective-permute-start.3 = (f32[4,18,1,1024]{3,2,1,0:T(1,128)}, f32[4,18,1,1024]{3,2,1,0:T(1,128)S(1)}, u32[]{:S(2)}, u32[]{:S(2)}) collective-permute-start(f32[4,18,1,1024]{3,2,1,0:T(1,128)} %get-tuple-element.9), channel_id=1, source_target_pairs={{8,0},{16,8},{24,16},{9,1},{17,9},{25,17},{10,2},{18,10},{26,18},{... | collective-permute-start | bytes 884744 | tf_op jit(solution)/shard_map/ppermute | solution.py:24
  86.1 63.1 %all-to-all-start.2 = ((f32[64,4,128]{2,1,0:T(4,128)}), f32[64,4,128]{2,1,0:T(4,128)}, u32[]{:S(2)}, u32[]{:S(2)}) async-start(f32[64,4,128]{2,1,0:T(4,128)} %bitcast.26), calls=%async_computation.2 | async-start | bytes 262144 | tf_op jit(solution)/shard_map/all_to_all | solution.py:166
  108.4 20.6 %collective-permute-start.4 = (f32[4,18,18,1]{2,0,3,1:T(4,128)S(1)}, f32[4,18,18,1]{2,0,3,1:T(4,128)S(1)}, u32[]{:S(2)}, u32[]{:S(2)}) collective-permute-start(f32[4,18,18,1]{2,0,3,1:T(4,128)S(1)} %copy.54), channel_id=1, source_target_pairs={{0,1},{1,2},{2,3},{3,4},{4,5},{5,6},{6,7},{8,9},{9,10},{10,11},{11... | collective-permute-start | bytes 15560 | tf_op jit(solution)/shard_map/ppermute | solution.py:21
  117.3 12.2 %collective-permute-start.5 = (f32[4,18,18,1]{2,0,3,1:T(4,128)S(1)}, f32[4,18,18,1]{2,0,3,1:T(4,128)S(1)}, u32[]{:S(2)}, u32[]{:S(2)}) collective-permute-start(f32[4,18,18,1]{2,0,3,1:T(4,128)S(1)} %copy.56), channel_id=1, source_target_pairs={{1,0},{2,1},{3,2},{4,3},{5,4},{6,5},{7,6},{9,8},{10,9},{11,10},{12... | collective-permute-start | bytes 15560 | tf_op jit(solution)/shard_map/ppermute | solution.py:24
  223.7 10.9 %collective-permute-start.20 = (f32[4,6,1]{2,1,0:T(8,128)S(1)}, f32[4,6,1]{2,1,0:T(8,128)S(1)}, u32[]{:S(2)}, u32[]{:S(2)}) collective-permute-start(f32[4,6,1]{2,1,0:T(8,128)S(1)} %get-tuple-element.49), channel_id=1, source_target_pairs={{0,1},{1,2},{2,3},{3,4},{4,5},{5,6},{6,7},{8,9},{9,10},{10,11},{11... | collective-permute-start | bytes 296 | tf_op jit(solution)/shard_map/ppermute | solution.py:21
  243.8 10.9 %collective-permute-start.24 = (f32[4,6,1]{2,1,0:T(8,128)S(1)}, f32[4,6,1]{2,1,0:T(8,128)S(1)}, u32[]{:S(2)}, u32[]{:S(2)}) collective-permute-start(f32[4,6,1]{2,1,0:T(8,128)S(1)} %get-tuple-element.47), channel_id=1, source_target_pairs={{0,1},{1,2},{2,3},{3,4},{4,5},{5,6},{6,7},{8,9},{9,10},{10,11},{11... | collective-permute-start | bytes 296 | tf_op jit(solution)/shard_map/ppermute | solution.py:21
  263.9 10.9 %collective-permute-start.28 = (f32[4,6,1]{2,1,0:T(8,128)S(1)}, f32[4,6,1]{2,1,0:T(8,128)S(1)}, u32[]{:S(2)}, u32[]{:S(2)}) collective-permute-start(f32[4,6,1]{2,1,0:T(8,128)S(1)} %get-tuple-element.45), channel_id=1, source_target_pairs={{0,1},{1,2},{2,3},{3,4},{4,5},{5,6},{6,7},{8,9},{9,10},{10,11},{11... | collective-permute-start | bytes 296 | tf_op jit(solution)/shard_map/ppermute | solution.py:21
  284.0 10.9 %collective-permute-start.32 = (f32[4,6,1]{2,1,0:T(8,128)S(1)}, f32[4,6,1]{2,1,0:T(8,128)S(1)}, u32[]{:S(2)}, u32[]{:S(2)}) collective-permute-start(f32[4,6,1]{2,1,0:T(8,128)S(1)} %get-tuple-element.43), channel_id=1, source_target_pairs={{0,1},{1,2},{2,3},{3,4},{4,5},{5,6},{6,7},{8,9},{9,10},{10,11},{11... | collective-permute-start | bytes 296 | tf_op jit(solution)/shard_map/ppermute | solution.py:21
  304.1 11.1 %collective-permute-start.36 = (f32[4,6,1]{2,1,0:T(8,128)S(1)}, f32[4,6,1]{2,1,0:T(8,128)S(1)}, u32[]{:S(2)}, u32[]{:S(2)}) collective-permute-start(f32[4,6,1]{2,1,0:T(8,128)S(1)} %get-tuple-element.41), channel_id=1, source_target_pairs={{0,1},{1,2},{2,3},{3,4},{4,5},{5,6},{6,7},{8,9},{9,10},{10,11},{11... | collective-permute-start | bytes 296 | tf_op jit(solution)/shard_map/ppermute | solution.py:21
  340.1 17.3 %collective-permute-start.42 = (f32[18,18,1]{2,1,0:T(8,128)S(1)}, f32[18,18,1]{2,1,0:T(8,128)S(1)}, u32[]{:S(2)}, u32[]{:S(2)}) collective-permute-start(f32[18,18,1]{2,1,0:T(8,128)S(1)} %get-tuple-element.18), channel_id=1, source_target_pairs={{1,0},{2,1},{3,2},{4,3},{5,4},{6,5},{7,6},{9,8},{10,9},{11,10},{12... | collective-permute-start | bytes 3896 | tf_op jit(solution)/shard_map/ppermute | solution.py:24
  349.2 23.9 %collective-permute-start.43 = (f32[18,18,1]{2,1,0:T(8,128)S(1)}, f32[18,18,1]{2,1,0:T(8,128)S(1)}, u32[]{:S(2)}, u32[]{:S(2)}) collective-permute-start(f32[18,18,1]{2,1,0:T(8,128)S(1)} %get-tuple-element.19), channel_id=1, source_target_pairs={{0,1},{1,2},{2,3},{3,4},{4,5},{5,6},{6,7},{8,9},{9,10},{10,11},{11... | collective-permute-start | bytes 3896 | tf_op jit(solution)/shard_map/ppermute | solution.py:21
  393.2 21.9 %collective-permute-start.48 = (f32[18,18,1]{2,1,0:T(8,128)S(1)}, f32[18,18,1]{2,1,0:T(8,128)S(1)}, u32[]{:S(2)}, u32[]{:S(2)}) collective-permute-start(f32[18,18,1]{2,1,0:T(8,128)S(1)} %get-tuple-element.16), channel_id=1, source_target_pairs={{1,0},{2,1},{3,2},{4,3},{5,4},{6,5},{7,6},{9,8},{10,9},{11,10},{12... | collective-permute-start | bytes 3896 | tf_op jit(solution)/shard_map/ppermute | solution.py:24
  402.2 22.6 %collective-permute-start.49 = (f32[18,18,1]{2,1,0:T(8,128)S(1)}, f32[18,18,1]{2,1,0:T(8,128)S(1)}, u32[]{:S(2)}, u32[]{:S(2)}) collective-permute-start(f32[18,18,1]{2,1,0:T(8,128)S(1)} %get-tuple-element.17), channel_id=1, source_target_pairs={{0,1},{1,2},{2,3},{3,4},{4,5},{5,6},{6,7},{8,9},{9,10},{10,11},{11... | collective-permute-start | bytes 3896 | tf_op jit(solution)/shard_map/ppermute | solution.py:21
  445.4 21.6 %collective-permute-start.54 = (f32[18,18,1]{2,1,0:T(8,128)S(1)}, f32[18,18,1]{2,1,0:T(8,128)S(1)}, u32[]{:S(2)}, u32[]{:S(2)}) collective-permute-start(f32[18,18,1]{2,1,0:T(8,128)S(1)} %get-tuple-element.14), channel_id=1, source_target_pairs={{1,0},{2,1},{3,2},{4,3},{5,4},{6,5},{7,6},{9,8},{10,9},{11,10},{12... | collective-permute-start | bytes 3896 | tf_op jit(solution)/shard_map/ppermute | solution.py:24
  454.0 22.8 %collective-permute-start.55 = (f32[18,18,1]{2,1,0:T(8,128)S(1)}, f32[18,18,1]{2,1,0:T(8,128)S(1)}, u32[]{:S(2)}, u32[]{:S(2)}) collective-permute-start(f32[18,18,1]{2,1,0:T(8,128)S(1)} %get-tuple-element.15), channel_id=1, source_target_pairs={{0,1},{1,2},{2,3},{3,4},{4,5},{5,6},{6,7},{8,9},{9,10},{10,11},{11... | collective-permute-start | bytes 3896 | tf_op jit(solution)/shard_map/ppermute | solution.py:21
  497.3 13.0 %collective-permute-start.60 = (f32[18,18,1]{2,1,0:T(8,128)S(1)}, f32[18,18,1]{2,1,0:T(8,128)S(1)}, u32[]{:S(2)}, u32[]{:S(2)}) collective-permute-start(f32[18,18,1]{2,1,0:T(8,128)S(1)} %get-tuple-element.12), channel_id=1, source_target_pairs={{1,0},{2,1},{3,2},{4,3},{5,4},{6,5},{7,6},{9,8},{10,9},{11,10},{12... | collective-permute-start | bytes 3896 | tf_op jit(solution)/shard_map/ppermute | solution.py:24
  499.7 20.9 %collective-permute-start.61 = (f32[18,18,1]{2,1,0:T(8,128)S(1)}, f32[18,18,1]{2,1,0:T(8,128)S(1)}, u32[]{:S(2)}, u32[]{:S(2)}) collective-permute-start(f32[18,18,1]{2,1,0:T(8,128)S(1)} %get-tuple-element.13), channel_id=1, source_target_pairs={{0,1},{1,2},{2,3},{3,4},{4,5},{5,6},{6,7},{8,9},{9,10},{10,11},{11... | collective-permute-start | bytes 3896 | tf_op jit(solution)/shard_map/ppermute | solution.py:21
  (72 other events, 817.5 us)
where the time goes:
time: 529 us; the launch traced here: 526 us
  starting transfers between devices  276 us (52%)
  waiting for transfers between devices  132 us (25%)
  other arithmetic  57.9 us (11%)
  local copies, waits for them, and re-layouts  56.6 us (11%)
    ppermute x31, starting transfers between devices, padded_2(): lax.ppermute(lax.slice_in_dim(block, 0, width, axis=dim), axis, backward)  147 us
    ppermute x31, starting transfers between devices, padded_2(): lax.ppermute(lax.slice_in_dim(block, block.shape[dim] - width, None, axis...  92.5 us
    ppermute x31, waiting for transfers between devices, padded_2(): lax.ppermute(lax.slice_in_dim(block, 0, width, axis=dim), axis, backward)  67.6 us
    ppermute x31, waiting for transfers between devices, padded_2(): lax.ppermute(lax.slice_in_dim(block, block.shape[dim] - width, None, axis...  64.7 us
    all_to_all x1, starting transfers between devices, per_device(): lax.all_to_all(tags.reshape(senders, capacity), ('gx', 'grp'), split_axis...  13.6 us
    all_to_all x1, starting transfers between devices, per_device(): lax.all_to_all(returned.reshape(senders, capacity, 128), ('gx', 'grp'), s...  12.9 us
    add x3, other arithmetic, per_device(): delta = delta + RELAXATION * (-resid - applied) / diagonal  11.9 us
    unnamed x68, local copies, waits for them, and re-layouts  11.4 us
  transfers between devices with their start and end apart: 65, of which 35 were waited for; matrix products, arithmetic and copies ran while one was open for 12% of the time, Pallas kernels for 0%

commit v1 on v0

v1 whole, which is shorter than its diff:
```python
import jax
import jax.numpy as jnp
from jax import lax
from jax.experimental import pallas as pl
from jax.experimental.pallas import tpu as pltpu
from jax.sharding import PartitionSpec as P

MESH = pl.DeviceIdType.MESH
F32 = jnp.float32
RELAX = 0.7
KEEP = 1.0 - RELAX
NGX, NGY, NGRP = 8, 4, 8
HIGH = lax.Precision.HIGHEST


def iota(shape, dim):
    return lax.broadcasted_iota(jnp.int32, shape, dim)


def nt(a, b):
    return lax.dot_general(
        a, b, (((1,), (1,)), ((), ())), precision=HIGH, preferred_element_type=F32
    )


def nn(a, b):
    return jnp.dot(a, b, precision=HIGH, preferred_element_type=F32)


def rcp(x):
    r = pl.reciprocal(x, approx=True)
    return r * (2.0 - x * r)


def harm(a, b):
    return 2.0 * a * b * rcp(a + b)


def z_below(v):
    r = pltpu.roll(v, 1, 2)
    return jnp.where(iota(v.shape, 2) == 0, pltpu.roll(r, 1, 1), r)


def z_above(v):
    r = pltpu.roll(v, 127, 2)
    return jnp.where(iota(v.shape, 2) == 127, pltpu.roll(r, 7, 1), r)


def kernel(
    cb_s,
    p_hbm,
    po_hbm,
    ac_hbm,
    k_hbm,
    cb_v,
    ow_v,
    cw_v,
    wi_v,
    rate_v,
    stor_v,
    old_v,
    out_hbm,
    bhp_out,
    PG,
    PP,
    PO,
    AC,
    KX,
    KY,
    KZ,
    AXL,
    AXH,
    AYL,
    AYH,
    AZL,
    AZH,
    CC,
    BB,
    D,
    OUT,
    OH,
    PR,
    OWN,
    W1,
    W2,
    HZP,
    HZK,
    ZS0,
    ZI,
    ZSD,
    ZR,
    CQ,
    CSO,
    CBO,
    CS,
    CB,
    VO,
    VX,
    lsem,
    a1s,
    a1r,
    a2s,
    a2r,
    ihs,
    ihr,
    css,
    csr,
    cbs,
    cbr,
    vxs,
    vxr,
    sws,
    swr,
):
    i = lax.axis_index("gx")
    j = lax.axis_index("gy")
    l = lax.axis_index("grp")
    i_lo, i_hi = lax.rem(i + NGX - 1, NGX), lax.rem(i + 1, NGX)
    l_lo, l_hi = lax.rem(l + NGRP - 1, NGRP), lax.rem(l + 1, NGRP)

    def rdma(src, dst, ss, rs, dev):
        return pltpu.make_async_remote_copy(
            src_ref=src, dst_ref=dst, send_sem=ss, recv_sem=rs, device_id=dev, device_id_type=MESH
        )

    load_g = pltpu.make_async_copy(p_hbm, PG, lsem.at[0])
    load_g.start()

    def load(ys, _):
        for yt in range(2):
            y = yt * 8 + ys
            pltpu.make_async_copy(
                p_hbm.at[:, yt, :, ys, :], PP.at[pl.ds(1, 16), 1 + y], lsem.at[1]
            ).start()
            pltpu.make_async_copy(
                k_hbm.at[0, :, yt, :, ys, :], KX.at[pl.ds(1, 16), y], lsem.at[2]
            ).start()
            pltpu.make_async_copy(
                k_hbm.at[1, :, yt, :, ys, :], KY.at[:, 1 + y], lsem.at[3]
            ).start()
            pltpu.make_async_copy(k_hbm.at[2, :, yt, :, ys, :], KZ.at[:, y], lsem.at[4]).start()
            pltpu.make_async_copy(po_hbm.at[:, yt, :, ys, :], PO.at[:, y], lsem.at[5]).start()
            pltpu.make_async_copy(ac_hbm.at[:, yt, :, ys, :], AC.at[:, y], lsem.at[6]).start()
        return 0

    lax.fori_loop(0, 8, load, 0)

    zplane = jnp.zeros((16, 8, 128), F32)

    @pl.when(j == 0)
    def _():
        PP[pl.ds(1, 16), 0] = zplane
        for s in range(1, 4):
            D[s, pl.ds(1, 16), 0] = zplane

    @pl.when(j == NGY - 1)
    def _():
        PP[pl.ds(1, 16), 17] = zplane
        for s in range(1, 4):
            D[s, pl.ds(1, 16), 17] = zplane

    bar = pltpu.get_barrier_semaphore()

    def greet(dev):
        pl.semaphore_signal(bar, inc=1, device_id=dev, device_id_type=MESH)

    for d in range(1, NGX):
        greet({"gx": lax.rem(i + d, NGX)})
    for d in range(1, NGRP):
        greet({"grp": lax.rem(l + d, NGRP)})
    for dj in range(1, NGY):
        for dz in range(3):
            greet({"gy": lax.rem(j + dj, NGY), "grp": lax.rem(l + dz + NGRP - 1, NGRP)})

    load_g.wait()

    def gather(g, _):
        for u in range(8):
            b = cb_s[0, g * 8 + u]
            x, y, k = b // 128, lax.rem(b // 8, 16), lax.rem(b, 8)
            PR[pl.ds(g * 8 + u, 1), :] = PG[x, y // 8, k, pl.ds(lax.rem(y, 8), 1), :]
        return 0

    lax.fori_loop(0, 16, gather, 0)
    wi = wi_v[...]
    sub = iota((8, 128), 0)
    lane = iota((8, 128), 1)
    sub128 = iota((128, 128), 0)
    lane128 = iota((128, 128), 1)
    ones8 = jnp.ones((8, 128), F32)
    weighted = nt(ones8, wi * PR[...])
    total = nt(ones8, wi)
    cb = cb_v[...]
    q = ow_v[...] * 8 + cw_v[...]
    q_hi, q_lo = q // 128, lax.rem(q, 128)
    pick = (sub128 == q_lo).astype(F32)
    share = nt(
        jnp.where(sub == q_hi, weighted, 0.0) + jnp.where(sub == q_hi + 4, total, 0.0), pick
    )
    own = i * NGRP + l
    own_row, shift = own // 16, lax.rem(own, 16) * 8
    OWN[...] = jnp.zeros((8, 128), F32)
    OWN[0:1, 0:8] = stor_v[...] * old_v[...] - rate_v[...]
    OWN[1:2, 0:8] = stor_v[...]
    placed = pltpu.roll(OWN[...], shift, 1)
    share = (
        share
        + jnp.where(sub == own_row, placed[0:1], 0.0)
        + jnp.where(sub == own_row + 4, placed[1:2], 0.0)
    )
    W1[i] = share

    def face_matrix(lo_ref, hi_ref, half, base, width):
        los, his = [], []
        for xx in range(8):
            row = base + (half * 8 + xx) * width * 8
            los.append(lo_ref[pl.ds(row, 16, stride=8), :])
            his.append(hi_ref[pl.ds(row + 7, 16, stride=8), :])
        return jnp.where(
            lane128 < 64, jnp.concatenate(los, axis=0), jnp.concatenate(his, axis=0)
        )

    def face_rows(lo_ref, hi_ref, half, base, width):
        t = jnp.transpose(face_matrix(lo_ref, hi_ref, half, base, width))
        return t[0:8], t[120:128]

    def spread(lo, hi):
        return jnp.transpose(
            jnp.where(sub128 == 0, lo, jnp.where(sub128 == 127, hi, 0.0))
        )

    PP2 = PP.reshape(18 * 18 * 8, 128)
    KZ2 = KZ.reshape(2048, 128)
    for ref, hbm, sem in ((PP.at[pl.ds(1, 16), pl.ds(1, 16)], KZ, 1), (KZ, KZ, 4)):
        pltpu.make_async_copy(KZ, ref, lsem.at[sem]).wait()
    for half in range(2):
        a, b = face_rows(PP2, PP2, half, 19 * 8, 18)
        ZS0[0, 0, half] = a
        ZS0[1, 0, half] = b
        a, b = face_rows(KZ2, KZ2, half, 0, 16)
        ZS0[0, 1, half] = a
        ZS0[1, 1, half] = b
    pltpu.make_async_copy(KZ, KX.at[pl.ds(1, 16)], lsem.at[2]).wait()
    pltpu.make_async_copy(KZ, KY.at[:, pl.ds(1, 16)], lsem.at[3]).wait()

    pl.semaphore_wait(bar, 23)

    sends = []
    for d in range(1, NGX):
        c = rdma(W1.at[i], W1.at[i], a1s.at[d], a1r.at[i], {"gx": lax.rem(i + d, NGX)})
        c.start()
        sends.append(c)

    inner = pl.ds(1, 16)
    zc_lo = rdma(ZS0.at[0], ZI.at[1], ihs.at[0], ihr.at[0], {"grp": l_lo})
    zc_hi = rdma(ZS0.at[1], ZI.at[0], ihs.at[1], ihr.at[1], {"grp": l_hi})
    zc_lo.start()
    zc_hi.start()
    xs = [
        rdma(KX.at[1], KX.at[17], ihs.at[2], ihr.at[2], {"gx": i_lo}),
        rdma(KX.at[16], KX.at[0], ihs.at[3], ihr.at[3], {"gx": i_hi}),
        rdma(PP.at[1, inner], PP.at[17, inner], ihs.at[4], ihr.at[4], {"gx": i_lo}),
        rdma(PP.at[16, inner], PP.at[0, inner], ihs.at[5], ihr.at[5], {"gx": i_hi}),
    ]
    for c in xs:
        c.start()
    y_down = [
        rdma(KY.at[:, 1], KY.at[:, 17], ihs.at[6], ihr.at[6], {"gy": lax.max(j - 1, 0)}),
        rdma(PP.at[inner, 1], PP.at[inner, 17], ihs.at[7], ihr.at[7], {"gy": lax.max(j - 1, 0)}),
    ]
    y_up = [
        rdma(KY.at[:, 16], KY.at[:, 0], ihs.at[8], ihr.at[8], {"gy": lax.min(j + 1, 3)}),
        rdma(PP.at[inner, 16], PP.at[inner, 0], ihs.at[9], ihr.at[9], {"gy": lax.min(j + 1, 3)}),
    ]

    @pl.when(j > 0)
    def _():
        for c in y_down:
            c.start()

    @pl.when(j < NGY - 1)
    def _():
        for c in y_up:
            c.start()

    def onehot(x, _):
        OH[x] = (sub128 + x * 128 == cb).astype(F32).astype(jnp.bfloat16)
        return 0

    lax.fori_loop(0, 16, onehot, 0)

    def halves(v):
        hi = v.astype(jnp.bfloat16)
        lo = (v - hi.astype(F32)).astype(jnp.bfloat16)
        return jnp.concatenate([hi, lo], axis=1)

    def blocks(x, parts):
        r = jnp.dot(OH[x], parts, preferred_element_type=F32)
        return (r[:, :128] + r[:, 128:]).reshape(16, 8, 128)

    wi_parts = halves(wi)

    for d in range(1, NGX):
        s = lax.rem(i + d, NGX)
        rdma(W1.at[i], W1.at[s], a1s.at[d], a1r.at[s], {"gx": s}).wait_recv()
    acc8 = W1[0]
    for s in range(1, NGX):
        acc8 = acc8 + W1[s]
    W2[l] = acc8
    for d in range(1, NGRP):
        c = rdma(W2.at[l], W2.at[l], a2s.at[d], a2r.at[l], {"grp": lax.rem(l + d, NGRP)})
        c.start()
        sends.append(c)

    CQ[...] = jnp.zeros((8, 16, 8, 128), F32)
    pltpu.make_async_copy(KZ, PO, lsem.at[5]).wait()
    pltpu.make_async_copy(KZ, AC, lsem.at[6]).wait()
    for c in xs:
        c.wait_recv()

    @pl.when(j > 0)
    def _():
        for c in y_up:
            c.wait_recv()

    @pl.when(j < NGY - 1)
    def _():
        for c in y_down:
            c.wait_recv()

    zc_lo.wait_recv()
    zc_hi.wait_recv()

    @pl.when(i == 0)
    def _():
        KX[0] = zplane

    @pl.when(i == NGX - 1)
    def _():
        KX[17] = zplane

    @pl.when(j == 0)
    def _():
        KY[:, 0] = zplane

    @pl.when(j == NGY - 1)
    def _():
        KY[:, 17] = zplane

    has_lo = (l > 0).astype(F32)
    has_hi = (l < NGRP - 1).astype(F32)
    for half in range(2):
        rows = pl.ds(half * 128, 128)
        HZP[rows] = spread(ZI[0, 0, half][7:8], ZI[1, 0, half][0:1])
        HZK[rows] = spread(ZI[0, 1, half][7:8] * has_lo, ZI[1, 1, half][0:1] * has_hi)

    sh3 = (8, 8, 128)
    first = (iota(sh3, 2) == 0) & (iota(sh3, 1) == 0)
    last = (iota(sh3, 2) == 127) & (iota(sh3, 1) == 7)

    def column(ref, n):
        return jnp.concatenate(
            [jnp.broadcast_to(ref[pl.ds(n + u, 1), :], (8, 128))[None] for u in range(8)], axis=0
        )

    def operator(x, _):
        w16 = blocks(x, wi_parts)
        big = x // 4
        f_lo = (lax.rem(x, 4) == 0).astype(F32)
        f_hi = (lax.rem(x, 4) == 3).astype(F32)
        for yt in range(2):
            y0 = yt * 8
            c8 = pl.ds(y0, 8)
            kx = KX[x + 1, c8]
            txl, txh = harm(KX[x, c8], kx), harm(kx, KX[x + 2, c8])
            ky = KY[x, pl.ds(y0 + 1, 8)]
            tyl, tyh = harm(KY[x, c8], ky), harm(ky, KY[x, pl.ds(y0 + 2, 8)])
            kz = KZ[x, c8]
            hk = column(HZK, x * 16 + y0)
            tzl = harm(jnp.where(first, hk, z_below(kz)), kz)
            tzh = harm(kz, jnp.where(last, hk, z_above(kz)))
            tsum = ((txl + txh) + (tyl + tyh)) + (tzl + tzh)
            p = PP[x + 1, pl.ds(y0 + 1, 8)]
            hp = column(HZP, x * 16 + y0)
            nb = (
                (txl * PP[x, pl.ds(y0 + 1, 8)] + txh * PP[x + 2, pl.ds(y0 + 1, 8)])
                + (tyl * PP[x + 1, c8] + tyh * PP[x + 1, pl.ds(y0 + 2, 8)])
                + (
                    tzl * jnp.where(first, hp, z_below(p))
                    + tzh * jnp.where(last, hp, z_above(p))
                )
            )
            acc = AC[x, c8]
            w = w16[y0 : y0 + 8]
            r0 = acc * (p - PO[x, c8]) + tsum * p - nb + w * p
            accw = acc + w
            c = RELAX * rcp(accw + tsum)
            AXL[x, c8] = c * txl
            AXH[x, c8] = c * txh
            AYL[x, c8] = c * tyl
            AYH[x, c8] = c * tyh
            AZL[x, c8] = c * tzl
            AZH[x, c8] = c * tzh
            CC[x, c8] = c
            BB[x, c8] = -c * r0
            for yl in range(2):
                n = big * 4 + yt * 2 + yl
                part = slice(yl * 4, yl * 4 + 4)
                CQ[0, n] += r0[part].sum(0)
                CQ[1, n] += accw[part].sum(0)
                CQ[2, n] += txl[part].sum(0) * f_lo
                CQ[3, n] += txh[part].sum(0) * f_hi
                CQ[4, n] += tyl[yl * 4]
                CQ[5, n] += tyh[yl * 4 + 3]
                CQ[6, n] += tzl[part].sum(0)
                CQ[7, n] += tzh[part].sum(0)
        return 0

    lax.fori_loop(0, 16, operator, 0)

    sh4 = (16, 8, 128)
    lane4 = iota(sh4, 2)
    place4 = lane4 == (iota(sh4, 0) // 4) * 32 + iota(sh4, 1)

    def coarse_of(n):
        v = CQ[n]
        if n == 6:
            v = jnp.where(lane4 == 0, v, 0.0)
        if n == 7:
            v = jnp.where(lane4 == 127, v, 0.0)
        v = jnp.where(place4, jnp.sum(v, axis=2, keepdims=True), 0.0)
        v = ((v[0:4] + v[4:8]) + (v[8:12] + v[12:16])).sum(1, keepdims=True)
        out = jnp.zeros((8, 128), F32)
        for y in range(4):
            out = jnp.where(lax.rem(sub, 4) == y, v[y], out)
        return out

    r_c, a_c, xl, xh, yl, yh, zl, zh = [coarse_of(n) for n in range(8)]
    used = lax.rem(lane, 32) < 8
    diag_c = jnp.where(used, a_c + ((xl + xh) + (yl + yh)) + (zl + zh), 1.0)
    scale = jnp.where(used, RELAX / diag_c, 0.0)
    CSO[0] = jnp.where(lane >= 32, scale * xl, 0.0)
    CSO[1] = jnp.where(lane < 96, scale * xh, 0.0)
    CSO[2] = scale * yl
    CSO[3] = scale * yh
    CSO[4] = scale * zl
    CSO[5] = scale * zh
    peers = [(dj, dz) for dj in range(NGY) for dz in range(3) if (dj, dz) != (0, 1)]

    def to_peers(own_ref, all_ref, ss, rs):
        for n, (dj, dz) in enumerate(peers):
            dev = {"gy": lax.rem(j + dj, NGY), "grp": lax.rem(l + dz + NGRP - 1, NGRP)}
            c = rdma(own_ref, all_ref.at[2 - dz, j], ss.at[n], rs.at[2 - dz, j], dev)
            c.start()
            sends.append(c)

    def from_peers(own_ref, all_ref, ss, rs):
        for n, (dj, dz) in enumerate(peers):
            s = lax.rem(j + dj, NGY)
            dev = {"gy": s, "grp": lax.rem(l + dz + NGRP - 1, NGRP)}
            rdma(own_ref, all_ref.at[dz, s], ss.at[n], rs.at[dz, s], dev).wait_recv()

    to_peers(CSO, CS, css, csr)
    CS[1, j] = CSO[...]

    AZL2 = AZL.reshape(2048, 128)
    AZH2 = AZH.reshape(2048, 128)
    end_coef = []
    for half in range(2):
        a, b = face_rows(AZL2, AZH2, half, 0, 16)
        end_coef.append((a[0:1], b[7:8]))

    for d in range(1, NGRP):
        s = lax.rem(l + d, NGRP)
        rdma(W2.at[l], W2.at[s], a2s.at[d], a2r.at[s], {"grp": s}).wait_recv()
    acc8 = W2[0]
    for s in range(1, NGRP):
        acc8 = acc8 + W2[s]
    bhp = jnp.where(sub < 4, acc8 / jnp.where(sub < 4, pltpu.roll(acc8, 4, 0), 1.0), 0.0)
    mine = pltpu.roll(jnp.where(sub == own_row, bhp, 0.0), lax.rem(128 - shift, 128), 1)
    bhp_out[...] = jnp.sum(mine, axis=0, keepdims=True)[:, 0:8]
    bhp_c = jnp.sum(
        jnp.where(sub == q_hi, nn(bhp, pick), 0.0), axis=0, keepdims=True
    )

    cx, cy, ck = cb // 128, lax.rem(cb // 8, 16), lax.rem(cb, 8)
    spot = (sub128 == (cx // 4) * 32 + ck).astype(F32)
    flow = jnp.where(lax.rem(sub, 4) == cy // 4, total * bhp_c, 0.0)
    CBO[...] = scale * (nt(flow, spot) - r_c)
    to_peers(CBO, CB, cbs, cbr)
    CB[1, j] = CBO[...]

    bhp_col = jnp.sum(jnp.where(sub128 == lane128, bhp_c, 0.0), axis=1, keepdims=True)
    wb_parts = halves(wi * bhp_col)

    def finish(x, _):
        BB[x] = BB[x] + CC[x] * blocks(x, wb_parts)
        return 0

    lax.fori_loop(0, 16, finish, 0)

    def joined(tile):
        out = []
        for t in range(2):
            v = None
            for dz in range(3):
                u = jnp.where(sub < 4, tile(dz, 2 * t), tile(dz, 2 * t + 1))
                if dz:
                    u = pltpu.roll(u, 8 * dz, 1)
                v = u if v is None else v + u
            out.append(v)
        return jnp.concatenate(out, axis=0)

    from_peers(CSO, CS, css, csr)
    coef = [joined(lambda dz, g, n=n: CS[dz, g, n]) for n in range(6)]
    from_peers(CBO, CB, cbs, cbr)
    rhs = joined(lambda dz, g: CB[dz, g])

    def coarse_step(_, v):
        return (
            (KEEP * v + rhs)
            + (coef[0] * pltpu.roll(v, 32, 1) + coef[1] * pltpu.roll(v, 96, 1))
            + (coef[2] * pltpu.roll(v, 1, 0) + coef[3] * pltpu.roll(v, 15, 0))
            + (coef[4] * pltpu.roll(v, 1, 1) + coef[5] * pltpu.roll(v, 127, 1))
        )

    v = lax.fori_loop(0, 7, coarse_step, rhs)
    mine = jnp.zeros((8, 128), F32)
    for g in range(NGY):
        mine = jnp.where(j == g, pltpu.roll(v, (17 - 4 * g) % 16, 0)[0:8], mine)
    VO[...] = mine
    vx_lo = rdma(VO, VX.at[1], vxs.at[0], vxr.at[0], {"gx": i_lo})
    vx_hi = rdma(VO, VX.at[0], vxs.at[1], vxr.at[1], {"gx": i_hi})
    vx_lo.start()
    vx_hi.start()

    def upright(tile):
        return jnp.transpose(jnp.concatenate([tile] * 16, axis=0))

    def cell(up, big, row):
        t = jnp.where(lane == row, up[big * 32 + 8 : big * 32 + 16], 0.0)
        return jnp.broadcast_to(jnp.sum(t, axis=1, keepdims=True), (8, 128))

    up = upright(mine)
    for big in range(4):
        for row in range(6):
            t = cell(up, big, row)
            ys = (0,) if row == 0 else (17,) if row == 5 else range(row * 4 - 3, row * 4 + 1)
            for x in range(4):
                for y in ys:
                    D[0, 1 + big * 4 + x, y] = t
    for half in range(2):
        big = half * 2 + lane128 // 64
        row = 1 + lax.rem(lane, 16) // 4
        for n, at in ((0, 7), (1, 16)):
            u = nn(mine, (sub128 == big * 32 + at).astype(F32))
            u = jnp.sum(jnp.where(sub == row, u, 0.0), axis=0, keepdims=True)
            ZR[0, n, half] = jnp.broadcast_to(u, (8, 128))
    vx_lo.wait_recv()
    vx_hi.wait_recv()
    for n, big, at in ((0, 3, 0), (1, 0, 17)):
        up = upright(VX[n])
        for row in range(1, 5):
            t = cell(up, big, row)
            for y in range(row * 4 - 3, row * 4 + 1):
                D[0, at, y] = t

    def sweep(s, put):
        def body(x, _):
            for yt in range(2):
                y0 = yt * 8
                c8 = pl.ds(y0, 8)
                v = D[s, x + 1, pl.ds(y0 + 1, 8)]
                new = (
                    (KEEP * v + BB[x, c8])
                    + (
                        AXL[x, c8] * D[s, x, pl.ds(y0 + 1, 8)]
                        + AXH[x, c8] * D[s, x + 2, pl.ds(y0 + 1, 8)]
                    )
                    + (
                        AYL[x, c8] * D[s, x + 1, c8]
                        + AYH[x, c8] * D[s, x + 1, pl.ds(y0 + 2, 8)]
                    )
                    + (AZL[x, c8] * z_below(v) + AZH[x, c8] * z_above(v))
                )
                put(x, y0, new)
            return 0

        lax.fori_loop(0, 16, body, 0)

    D2 = D.reshape(4 * 18 * 18 * 8, 128)

    def base_of(s):
        return (s * 18 * 18 + 19) * 8

    def fix_ends(s, ref, base, width):
        for half in range(2):
            a, b = face_rows(D2, D2, half, base_of(s), 18)
            fix = spread(
                end_coef[half][0] * (ZR[s, 0, half][7:8] - b[7:8]),
                end_coef[half][1] * (ZR[s, 1, half][0:1] - a[0:1]),
            )
            lo = jnp.where(lane128 < 64, fix, 0.0)
            hi = fix - lo
            for xx in range(8):
                row = base + (half * 8 + xx) * width * 8
                at = pl.ds(row, 16, stride=8)
                ref[at, :] = ref[at, :] + lo[xx * 16 : xx * 16 + 16]
                at = pl.ds(row + 7, 16, stride=8)
                ref[at, :] = ref[at, :] + hi[xx * 16 : xx * 16 + 16]

    def exchange(s):
        out = [
            rdma(ZSD.at[s, 0], ZR.at[s, 1], sws.at[s, 0], swr.at[s, 0], {"grp": l_lo}),
            rdma(ZSD.at[s, 1], ZR.at[s, 0], sws.at[s, 1], swr.at[s, 1], {"grp": l_hi}),
            rdma(D.at[s, 1, inner], D.at[s, 17, inner], sws.at[s, 2], swr.at[s, 2], {"gx": i_lo}),
            rdma(D.at[s, 16, inner], D.at[s, 0, inner], sws.at[s, 3], swr.at[s, 3], {"gx": i_hi}),
        ]
        down = rdma(
            D.at[s, inner, 1],
            D.at[s, inner, 17],
            sws.at[s, 4],
            swr.at[s, 4],
            {"gy": lax.max(j - 1, 0)},
        )
        up = rdma(
            D.at[s, inner, 16],
            D.at[s, inner, 0],
            sws.at[s, 5],
            swr.at[s, 5],
            {"gy": lax.min(j + 1, 3)},
        )
        return out, down, up

    def step(s, _):
        def put(x, y0, new):
            D[s + 1, x + 1, pl.ds(y0 + 1, 8)] = new

        sweep(s, put)
        fix_ends(s, D2, base_of(s + 1), 18)
        for half in range(2):
            a, b = face_rows(D2, D2, half, base_of(s + 1), 18)
            ZSD[s + 1, 0, half] = a
            ZSD[s + 1, 1, half] = b
        out, down, up = exchange(s + 1)
        for c in out:
            c.start()

        @pl.when(j > 0)
        def _():
            down.start()

        @pl.when(j < NGY - 1)
        def _():
            up.start()

        for c in out:
            c.wait()

        @pl.when(j > 0)
        def _():
            down.wait_send()
            up.wait_recv()

        @pl.when(j < NGY - 1)
        def _():
            up.wait_send()
            down.wait_recv()

        return 0

    lax.fori_loop(0, 3, step, 0)

    def put_last(x, y0, new):
        OUT[x, y0 // 8] = PP[x + 1, pl.ds(y0 + 1, 8)] + new

    sweep(3, put_last)
    OUT2 = OUT.reshape(2048, 128)
    fix_ends(3, OUT2, 0, 16)

    def store(ys, _):
        pltpu.make_async_copy(OUT.at[:, :, ys], out_hbm.at[:, :, :, ys, :], lsem.at[0]).start()
        return 0

    lax.fori_loop(0, 8, store, 0)

    for c in sends + xs + [zc_lo, zc_hi, vx_lo, vx_hi]:
        c.wait_send()

    @pl.when(j > 0)
    def _():
        for c in y_down:
            c.wait_send()

    @pl.when(j < NGY - 1)
    def _():
        for c in y_up:
            c.wait_send()

    pltpu.make_async_copy(OUT, out_hbm, lsem.at[0]).wait()


def tiles(a):
    return a.reshape(16, 2, 8, 8, 128).transpose(0, 1, 3, 2, 4)


def per_device(
    pressure,
    pressure_old,
    accumulation,
    permeability,
    comp_block,
    comp_owner,
    comp_well,
    comp_wi,
    well_rate,
    well_storage,
    well_bhp_old,
):
    perm = permeability.reshape(3, 16, 2, 8, 8, 128).transpose(0, 1, 2, 4, 3, 5)
    hbm = pl.BlockSpec(memory_space=pl.ANY)
    vmem = pl.BlockSpec(memory_space=pltpu.VMEM)
    smem = pl.BlockSpec(memory_space=pltpu.SMEM)
    grid = (16, 16, 8, 128)
    dma = pltpu.SemaphoreType.DMA
    cb = comp_block.reshape(1, 128)

    def vm(*shape):
        return pltpu.VMEM(shape, F32)

    out, bhp = pl.pallas_call(
        kernel,
        out_shape=(
            jax.ShapeDtypeStruct((16, 2, 8, 8, 128), F32),
            jax.ShapeDtypeStruct((1, 8), F32),
        ),
        in_specs=[smem] + [hbm] * 4 + [vmem] * 7,
        out_specs=(hbm, vmem),
        scratch_shapes=[
            vm(16, 2, 8, 8, 128),
            vm(18, 18, 8, 128),
            vm(*grid),
            vm(*grid),
            vm(18, 16, 8, 128),
            vm(16, 18, 8, 128),
            vm(*grid),
            vm(*grid),
            vm(*grid),
            vm(*grid),
            vm(*grid),
            vm(*grid),
            vm(*grid),
            vm(*grid),
            vm(*grid),
            vm(4, 18, 18, 8, 128),
            vm(16, 2, 8, 8, 128),
            pltpu.VMEM((16, 128, 128), jnp.bfloat16),
            vm(128, 128),
            vm(8, 128),
            vm(8, 8, 128),
            vm(8, 8, 128),
            vm(256, 128),
            vm(256, 128),
            vm(2, 2, 2, 8, 128),
            vm(2, 2, 2, 8, 128),
            vm(4, 2, 2, 8, 128),
            vm(4, 2, 2, 8, 128),
            vm(8, 16, 8, 128),
            vm(6, 8, 128),
            vm(8, 128),
            vm(3, 4, 6, 8, 128),
            vm(3, 4, 8, 128),
            vm(8, 128),
            vm(2, 8, 128),
            dma((7,)),
            dma((8,)),
            dma((8,)),
            dma((8,)),
            dma((8,)),
            dma((10,)),
            dma((10,)),
            dma((11,)),
            dma((3, 4)),
            dma((11,)),
            dma((3, 4)),
            dma((2,)),
            dma((2,)),
            dma((4, 6)),
            dma((4, 6)),
        ],
        compiler_params=pltpu.CompilerParams(
            collective_id=0, has_side_effects=True, vmem_limit_bytes=60 * 1024 * 1024
        ),
    )(
        cb,
        tiles(pressure),
        tiles(pressure_old),
        tiles(accumulation),
        perm,
        cb,
        comp_owner.reshape(1, 128),
        comp_well.reshape(1, 128),
        comp_wi.reshape(128, 128),
        well_rate.reshape(1, 8),
        well_storage.reshape(1, 8),
        well_bhp_old.reshape(1, 8),
    )
    new = out.transpose(0, 1, 3, 2, 4).reshape(16, 16, 1024)
    return new, bhp.reshape(1, 1, 1, 8)


def solution(mesh):
    return jax.shard_map(
        per_device,
        mesh=mesh,
        in_specs=(
            P("gx", "gy", "grp"),
            P("gx", "gy", "grp"),
            P("gx", "gy", "grp"),
            P(None, "gx", "gy", "grp"),
            P("gx", "gy", "grp", None),
            P("gx", "gy", "grp", None, None),
            P("gx", "gy", "grp", None),
            P("gx", "gy", "grp", None, None),
            P("gx", "gy", "grp", None),
            P("gx", "gy", "grp", None),
            P("gx", "gy", "grp", None),
        ),
        out_specs=(P("gx", "gy", "grp"), P("gx", "gy", "grp", None)),
        check_vma=False,
    )
```

time: 529 us -> 71.2 us (0.13)
  the two profiles are of different devices: /device:TPU:46 before, /device:TPU:32 now
where the time goes in v1:
time: 71.2 us; the launch traced here: 71 us
  Pallas kernels  67 us (94%)
  local copies, waits for them, and re-layouts  3.42 us (5%)
    pallas_call x1, Pallas kernels, per_device(): pl.pallas_call(kernel, out_shape=(jax.ShapeDtypeStruct((16, 2, 8, 8, 128)...  67 us
    unnamed x2, local copies, waits for them, and re-layouts  3.42 us

profile of v1, /device:TPU:32, one launch (start us, length us, event | category | flops | bytes accessed | tf_op | source)
XLA Modules:
  0.0 71.0 jit_solution(15818146458750242868)
XLA Ops:
  0.6 67.0 %shard_map.122 = (f32[16,2,8,8,128]{4,3,2,1,0:T(8,128)}, f32[1,8]{1,0:T(1,128)}) custom-call(s32[1,128]{1,0:T(1,128)} %bitcast.29, f32[16,2,8,8,128]{4,3,2,1,0:T(8,128)} %bitcast.25, f32[16,2,8,8,128]{4,3,2,1,0:T(8,128)} %bitcast.26, f32[16,2,8,8,128]{4,3,2,1,0:T(8,128)} %bitcast.27, f32[3,16,2,8,8,128]{5,4,3,2,1,0:T(8,128)} %bitcast.23, s32[1,128]{1,0:T(1,128)} %bitcast.30, ...), custom_call_target="tpu_custom_call" | custom-call | tf_op jit(solution)/shard_map/pallas_call | solution.py:731
  67.6 2.3 %copy.15 = f32[16,16,1024]{2,1,0:T(8,128)} copy(f32[16,16,1024]{2,1,0:T(8,128)} %bitcast.24) | data formatting | bytes 2097152
  69.9 1.1 %copy.16 = f32[1,1,1,8]{3,2,1,0:T(1,128)} copy(f32[1,1,1,8]{3,2,1,0:T(1,128)} %bitcast.36) | data formatting | bytes 64

commit v2 on v1

--- a/solution.py
+++ b/solution.py
@@ -87,8 +87,19 @@
     HZK,
     ZS0,
     ZI,
-    ZSD,
-    ZR,
+    SA,
+    RA,
+    SB,
+    RB,
+    AE,
+    E,
+    EX,
+    EY,
+    EYS,
+    FA,
+    AR,
+    FR,
+    UU,
     CQ,
     CSO,
     CBO,
@@ -109,6 +120,8 @@
     cbr,
     vxs,
     vxr,
+    ras,
+    rar,
     sws,
     swr,
 ):
@@ -122,6 +135,19 @@
         return pltpu.make_async_remote_copy(
             src_ref=src, dst_ref=dst, send_sem=ss, recv_sem=rs, device_id=dev, device_id_type=MESH
         )
+
+    bar = pltpu.get_barrier_semaphore()
+
+    def greet(dev):
+        pl.semaphore_signal(bar, inc=1, device_id=dev, device_id_type=MESH)
+
+    for d in range(1, NGX):
+        greet({"gx": lax.rem(i + d, NGX)})
+    for d in range(1, NGRP):
+        greet({"grp": lax.rem(l + d, NGRP)})
+    for dj in range(1, NGY):
+        for dz in range(3):
+            greet({"gy": lax.rem(j + dj, NGY), "grp": lax.rem(l + dz + NGRP - 1, NGRP)})
 
     load_g = pltpu.make_async_copy(p_hbm, PG, lsem.at[0])
     load_g.start()
@@ -144,33 +170,6 @@
         return 0
 
     lax.fori_loop(0, 8, load, 0)
-
-    zplane = jnp.zeros((16, 8, 128), F32)
-
-    @pl.when(j == 0)
-    def _():
-        PP[pl.ds(1, 16), 0] = zplane
-        for s in range(1, 4):
-            D[s, pl.ds(1, 16), 0] = zplane
-
-    @pl.when(j == NGY - 1)
-    def _():
-        PP[pl.ds(1, 16), 17] = zplane
-        for s in range(1, 4):
-            D[s, pl.ds(1, 16), 17] = zplane
-
-    bar = pltpu.get_barrier_semaphore()
-
-    def greet(dev):
-        pl.semaphore_signal(bar, inc=1, device_id=dev, device_id_type=MESH)
-
-    for d in range(1, NGX):
-        greet({"gx": lax.rem(i + d, NGX)})
-    for d in range(1, NGRP):
-        greet({"grp": lax.rem(l + d, NGRP)})
-    for dj in range(1, NGY):
-        for dz in range(3):
-            greet({"gy": lax.rem(j + dj, NGY), "grp": lax.rem(l + dz + NGRP - 1, NGRP)})
 
     load_g.wait()
 
@@ -210,39 +209,6 @@
     )
     W1[i] = share
 
-    def face_matrix(lo_ref, hi_ref, half, base, width):
-        los, his = [], []
-        for xx in range(8):
-            row = base + (half * 8 + xx) * width * 8
-            los.append(lo_ref[pl.ds(row, 16, stride=8), :])
-            his.append(hi_ref[pl.ds(row + 7, 16, stride=8), :])
-        return jnp.where(
-            lane128 < 64, jnp.concatenate(los, axis=0), jnp.concatenate(his, axis=0)
-        )
-
-    def face_rows(lo_ref, hi_ref, half, base, width):
-        t = jnp.transpose(face_matrix(lo_ref, hi_ref, half, base, width))
-        return t[0:8], t[120:128]
-
-    def spread(lo, hi):
-        return jnp.transpose(
-            jnp.where(sub128 == 0, lo, jnp.where(sub128 == 127, hi, 0.0))
-        )
-
-    PP2 = PP.reshape(18 * 18 * 8, 128)
-    KZ2 = KZ.reshape(2048, 128)
-    for ref, hbm, sem in ((PP.at[pl.ds(1, 16), pl.ds(1, 16)], KZ, 1), (KZ, KZ, 4)):
-        pltpu.make_async_copy(KZ, ref, lsem.at[sem]).wait()
-    for half in range(2):
-        a, b = face_rows(PP2, PP2, half, 19 * 8, 18)
-        ZS0[0, 0, half] = a
-        ZS0[1, 0, half] = b
-        a, b = face_rows(KZ2, KZ2, half, 0, 16)
-        ZS0[0, 1, half] = a
-        ZS0[1, 1, half] = b
-    pltpu.make_async_copy(KZ, KX.at[pl.ds(1, 16)], lsem.at[2]).wait()
-    pltpu.make_async_copy(KZ, KY.at[:, pl.ds(1, 16)], lsem.at[3]).wait()
-
     pl.semaphore_wait(bar, 23)
 
     sends = []
@@ -250,6 +216,53 @@
         c = rdma(W1.at[i], W1.at[i], a1s.at[d], a1r.at[i], {"gx": lax.rem(i + d, NGX)})
         c.start()
         sends.append(c)
+
+    zplane = jnp.zeros((16, 8, 128), F32)
+
+    @pl.when(j == 0)
+    def _():
+        PP[pl.ds(1, 16), 0] = zplane
+        for s in range(1, 4):
+            D[s, pl.ds(1, 16), 0] = zplane
+            EY[s, 0] = jnp.zeros((16, 128), F32)
+
+    @pl.when(j == NGY - 1)
+    def _():
+        PP[pl.ds(1, 16), 17] = zplane
+        for s in range(1, 4):
+            D[s, pl.ds(1, 16), 17] = zplane
+            EY[s, 1] = jnp.zeros((16, 128), F32)
+
+    lane64 = iota((64, 128), 1)
+
+    def end_rows(ref, part, k, base, width):
+        return jnp.concatenate(
+            [
+                ref[pl.ds(base + (part * 4 + u) * width * 8 + k, 16, stride=8), :]
+                for u in range(4)
+            ],
+            axis=0,
+        )
+
+    def pack_ends(refs, lo_ref, hi_ref):
+        lo = hi = jnp.zeros((64, 128), F32)
+        for part in range(4):
+            for n, (ref, base, width) in enumerate(refs):
+                to = part * 32 + n * 4
+                a = jnp.where(lane64 < 4, end_rows(ref, part, 0, base, width), 0.0)
+                b = jnp.where(lane64 >= 124, end_rows(ref, part, 7, base, width), 0.0)
+                lo = lo + (pltpu.roll(a, to, 1) if to else a)
+                hi = hi + pltpu.roll(b, to + 4, 1)
+        lo_ref[...] = lo
+        hi_ref[...] = hi
+
+    PP2 = PP.reshape(18 * 18 * 8, 128)
+    KZ2 = KZ.reshape(2048, 128)
+    for ref, hbm, sem in ((PP.at[pl.ds(1, 16), pl.ds(1, 16)], KZ, 1), (KZ, KZ, 4)):
+        pltpu.make_async_copy(KZ, ref, lsem.at[sem]).wait()
+    pack_ends(((PP2, 19 * 8, 18), (KZ2, 0, 16)), ZS0.at[0], ZS0.at[1])
+    pltpu.make_async_copy(KZ, KX.at[pl.ds(1, 16)], lsem.at[2]).wait()
+    pltpu.make_async_copy(KZ, KY.at[:, pl.ds(1, 16)], lsem.at[3]).wait()
 
     inner = pl.ds(1, 16)
     zc_lo = rdma(ZS0.at[0], ZI.at[1], ihs.at[0], ihr.at[0], {"grp": l_lo})
@@ -349,10 +362,15 @@
 
     has_lo = (l > 0).astype(F32)
     has_hi = (l < NGRP - 1).astype(F32)
-    for half in range(2):
-        rows = pl.ds(half * 128, 128)
-        HZP[rows] = spread(ZI[0, 0, half][7:8], ZI[1, 0, half][0:1])
-        HZK[rows] = spread(ZI[0, 1, half][7:8] * has_lo, ZI[1, 1, half][0:1] * has_hi)
+    for part in range(4):
+        rows = pl.ds(part * 64, 64)
+        for n, ref in enumerate((HZP, HZK)):
+            at = part * 32 + n * 4
+            lo = pltpu.roll(ZI[0], (128 - at - 3) % 128, 1)
+            hi = pltpu.roll(ZI[1], 127 - at, 1)
+            if n:
+                lo, hi = lo * has_lo, hi * has_hi
+            ref[rows] = jnp.where(lane64 == 0, lo, hi)
 
     sh3 = (8, 8, 128)
     first = (iota(sh3, 2) == 0) & (iota(sh3, 1) == 0)
@@ -420,7 +438,7 @@
 
     sh4 = (16, 8, 128)
     lane4 = iota(sh4, 2)
-    place4 = lane4 == (iota(sh4, 0) // 4) * 32 + iota(sh4, 1)
+    place4 = lane4 == iota(sh4, 0) * 8 + iota(sh4, 1)
 
     def coarse_of(n):
         v = CQ[n]
@@ -429,22 +447,24 @@
         if n == 7:
             v = jnp.where(lane4 == 127, v, 0.0)
         v = jnp.where(place4, jnp.sum(v, axis=2, keepdims=True), 0.0)
-        v = ((v[0:4] + v[4:8]) + (v[8:12] + v[12:16])).sum(1, keepdims=True)
-        out = jnp.zeros((8, 128), F32)
-        for y in range(4):
-            out = jnp.where(lax.rem(sub, 4) == y, v[y], out)
-        return out
+        return jnp.sum(v.sum(0), axis=0, keepdims=True)
 
     r_c, a_c, xl, xh, yl, yh, zl, zh = [coarse_of(n) for n in range(8)]
-    used = lax.rem(lane, 32) < 8
-    diag_c = jnp.where(used, a_c + ((xl + xh) + (yl + yh)) + (zl + zh), 1.0)
-    scale = jnp.where(used, RELAX / diag_c, 0.0)
-    CSO[0] = jnp.where(lane >= 32, scale * xl, 0.0)
-    CSO[1] = jnp.where(lane < 96, scale * xh, 0.0)
-    CSO[2] = scale * yl
-    CSO[3] = scale * yh
-    CSO[4] = scale * zl
-    CSO[5] = scale * zh
+    scale = RELAX / (a_c + ((xl + xh) + (yl + yh)) + (zl + zh))
+    lane1 = iota((1, 128), 1)
+    CSO[...] = jnp.concatenate(
+        [
+            jnp.where(lane1 >= 32, scale * xl, 0.0),
+            jnp.where(lane1 < 96, scale * xh, 0.0),
+            scale * yl,
+            scale * yh,
+            scale * zl,
+            scale * zh,
+            scale,
+            scale,
+        ],
+        axis=0,
+    )
     peers = [(dj, dz) for dj in range(NGY) for dz in range(3) if (dj, dz) != (0, 1)]
 
     def to_peers(own_ref, all_ref, ss, rs):
@@ -463,12 +483,23 @@
     to_peers(CSO, CS, css, csr)
     CS[1, j] = CSO[...]
 
-    AZL2 = AZL.reshape(2048, 128)
-    AZH2 = AZH.reshape(2048, 128)
-    end_coef = []
-    for half in range(2):
-        a, b = face_rows(AZL2, AZH2, half, 0, 16)
-        end_coef.append((a[0:1], b[7:8]))
+    def flat(ref):
+        return (ref.reshape(2048, 128), 0, 16)
+
+    ends_s = [
+        rdma(SA.at[0], RA.at[1], ras.at[0], rar.at[0], {"grp": l_lo}),
+        rdma(SA.at[1], RA.at[0], ras.at[1], rar.at[1], {"grp": l_hi}),
+        rdma(SB.at[0], RB.at[1], ras.at[2], rar.at[2], {"grp": l_lo}),
+        rdma(SB.at[1], RB.at[0], ras.at[3], rar.at[3], {"grp": l_hi}),
+    ]
+    pack_ends([flat(r) for r in (AXL, AXH, AYL, AYH, AZL, AZH)], SA.at[0], SA.at[1])
+    ends_s[0].start()
+    ends_s[1].start()
+    AZL2, AZH2 = AZL.reshape(2048, 128), AZH.reshape(2048, 128)
+    for part in range(4):
+        AR[pl.ds(part * 64, 64)] = jnp.where(
+            lane64 < 64, end_rows(AZL2, part, 0, 0, 16), end_rows(AZH2, part, 7, 0, 16)
+        )
 
     for d in range(1, NGRP):
         s = lax.rem(l + d, NGRP)
@@ -484,9 +515,8 @@
     )
 
     cx, cy, ck = cb // 128, lax.rem(cb // 8, 16), lax.rem(cb, 8)
-    spot = (sub128 == (cx // 4) * 32 + ck).astype(F32)
-    flow = jnp.where(lax.rem(sub, 4) == cy // 4, total * bhp_c, 0.0)
-    CBO[...] = scale * (nt(flow, spot) - r_c)
+    spot = (sub128 == (cx // 4) * 32 + (cy // 4) * 8 + ck).astype(F32)
+    CBO[...] = scale * (nt(total * bhp_c, spot) - r_c)
     to_peers(CBO, CB, cbs, cbr)
     CB[1, j] = CBO[...]
 
@@ -498,23 +528,29 @@
         return 0
 
     lax.fori_loop(0, 16, finish, 0)
-
-    def joined(tile):
-        out = []
-        for t in range(2):
-            v = None
-            for dz in range(3):
-                u = jnp.where(sub < 4, tile(dz, 2 * t), tile(dz, 2 * t + 1))
-                if dz:
-                    u = pltpu.roll(u, 8 * dz, 1)
-                v = u if v is None else v + u
-            out.append(v)
-        return jnp.concatenate(out, axis=0)
-
+    pack_ends([flat(BB)], SB.at[0], SB.at[1])
+    ends_s[2].start()
+    ends_s[3].start()
+
+    def joined(all_ref):
+        block = lax.rem(lane, 32) // 8
+        for g in range(NGY):
+            for y in range(4):
+                u = None
+                for dz in range(3):
+                    t = all_ref[dz, g]
+                    to = (8 * (dz - y)) % 128
+                    t = pltpu.roll(t, to, 1) if to else t
+                    u = jnp.where(block == dz, t, 0.0 if u is None else u)
+                UU[g * 4 + y] = u
+
+    UU2 = UU.reshape(128, 128)
     from_peers(CSO, CS, css, csr)
-    coef = [joined(lambda dz, g, n=n: CS[dz, g, n]) for n in range(6)]
+    joined(CS)
+    coef = [UU2[pl.ds(n, 16, stride=8), :] for n in range(6)]
     from_peers(CBO, CB, cbs, cbr)
-    rhs = joined(lambda dz, g: CB[dz, g])
+    joined(CB)
+    rhs = UU2[pl.ds(0, 16, stride=8), :]
 
     def coarse_step(_, v):
         return (
@@ -549,13 +585,27 @@
             for x in range(4):
                 for y in ys:
                     D[0, 1 + big * 4 + x, y] = t
-    for half in range(2):
-        big = half * 2 + lane128 // 64
-        row = 1 + lax.rem(lane, 16) // 4
-        for n, at in ((0, 7), (1, 16)):
-            u = nn(mine, (sub128 == big * 32 + at).astype(F32))
-            u = jnp.sum(jnp.where(sub == row, u, 0.0), axis=0, keepdims=True)
-            ZR[0, n, half] = jnp.broadcast_to(u, (8, 128))
+    sub16 = iota((16, 128), 0)
+    y_lo = y_hi = jnp.zeros((16, 128), F32)
+    for big in range(4):
+        lo, hi = [
+            jnp.sum(jnp.where(lane == big * 32 + at, mine, 0.0), axis=1, keepdims=True)
+            for at in (7, 16)
+        ]
+        e = jnp.where(lane < 64, hi, lo)
+        rows = jnp.zeros((16, 128), F32)
+        for y in range(4):
+            rows = jnp.where(sub16 // 4 == y, e[y + 1 : y + 2], rows)
+        for u in range(4):
+            E[0, pl.ds((big * 4 + u) * 16, 16)] = rows
+        y_lo = jnp.where(sub16 // 4 == big, e[0:1], y_lo)
+        y_hi = jnp.where(sub16 // 4 == big, e[5:6], y_hi)
+    EY[0, 0] = y_lo
+    EY[0, 1] = y_hi
+    ex_lo = rdma(E.at[0, pl.ds(0, 16)], EX.at[0, 1], sws.at[0, 4], swr.at[0, 4], {"gx": i_lo})
+    ex_hi = rdma(E.at[0, pl.ds(240, 16)], EX.at[0, 0], sws.at[0, 5], swr.at[0, 5], {"gx": i_hi})
+    ex_lo.start()
+    ex_hi.start()
     vx_lo.wait_recv()
     vx_hi.wait_recv()
     for n, big, at in ((0, 3, 0), (1, 0, 17)):
@@ -565,118 +615,193 @@
             for y in range(row * 4 - 3, row * 4 + 1):
                 D[0, at, y] = t
 
-    def sweep(s, put):
-        def body(x, _):
-            for yt in range(2):
-                y0 = yt * 8
-                c8 = pl.ds(y0, 8)
-                v = D[s, x + 1, pl.ds(y0 + 1, 8)]
-                new = (
-                    (KEEP * v + BB[x, c8])
-                    + (
-                        AXL[x, c8] * D[s, x, pl.ds(y0 + 1, 8)]
-                        + AXH[x, c8] * D[s, x + 2, pl.ds(y0 + 1, 8)]
-                    )
-                    + (
-                        AYL[x, c8] * D[s, x + 1, c8]
-                        + AYH[x, c8] * D[s, x + 1, pl.ds(y0 + 2, 8)]
-                    )
-                    + (AZL[x, c8] * z_below(v) + AZH[x, c8] * z_above(v))
+    D2 = D.reshape(4 * 18 * 18 * 8, 128)
+    E2 = E.reshape(4 * 256, 128)
+
+    def faces(s):
+        for part in range(4):
+            base = (s * 18 * 18 + 19) * 8
+            rows = pl.ds(part * 64, 64)
+            m = jnp.where(
+                lane64 < 64, end_rows(D2, part, 0, base, 18), end_rows(D2, part, 7, base, 18)
+            )
+            FA[rows] = m
+            d = E[s, rows] - m
+            FR[rows] = AR[rows] * jnp.where(
+                lane64 < 64, pltpu.roll(d, 1, 1), pltpu.roll(d, 127, 1)
+            )
+
+    def columns(s, x, y0, n):
+        at = pl.ds(y0, n)
+        v = D[s, x + 1, pl.ds(y0 + 1, n)]
+        shape = (n, 8, 128)
+        k, z = iota(shape, 1), iota(shape, 2)
+        ends = ((k == 0) & (z == 0)) | ((k == 7) & (z == 127))
+        fix = jnp.concatenate(
+            [
+                jnp.broadcast_to(FR[pl.ds(x * 16 + y0 + u, 1), :], (8, 128))[None]
+                for u in range(n)
+            ],
+            axis=0,
+        )
+        return (
+            (KEEP * v + BB[x, at])
+            + (
+                AXL[x, at] * D[s, x, pl.ds(y0 + 1, n)]
+                + AXH[x, at] * D[s, x + 2, pl.ds(y0 + 1, n)]
+            )
+            + (AYL[x, at] * D[s, x + 1, at] + AYH[x, at] * D[s, x + 1, pl.ds(y0 + 2, n)])
+            + (AZL[x, at] * z_below(v) + AZH[x, at] * z_above(v))
+            + jnp.where(ends, fix, 0.0)
+        )
+
+    def beyond(s):
+        shape = (4, 16, 128)
+        y, z = iota(shape, 1), iota(shape, 2)
+
+        def each_y(ref, part):
+            return jnp.concatenate(
+                [
+                    jnp.broadcast_to(ref[pl.ds(part * 4 + u, 1), :], (16, 128))[None]
+                    for u in range(4)
+                ],
+                axis=0,
+            )
+
+        for part in range(4):
+            rows = pl.ds(part * 64, 64)
+            e = E[s, rows].reshape(shape)
+            if part == 0:
+                left = jnp.concatenate([EX[s, 0], E[s, pl.ds(0, 48)]], axis=0)
+            else:
+                left = E[s, pl.ds(part * 64 - 16, 64)]
+            if part == 3:
+                right = jnp.concatenate([E[s, pl.ds(208, 48)], EX[s, 1]], axis=0)
+            else:
+                right = E[s, pl.ds(part * 64 + 16, 64)]
+            a = [AE[n, rows].reshape(shape) for n in range(7)]
+            m = FA[rows].reshape(shape)
+            new = (
+                (KEEP * e + a[6])
+                + (a[0] * left.reshape(shape) + a[1] * right.reshape(shape))
+                + (
+                    a[2] * jnp.where(y == 0, each_y(EY.at[s, 0], part), pltpu.roll(e, 1, 1))
+                    + a[3] * jnp.where(y == 15, each_y(EY.at[s, 1], part), pltpu.roll(e, 15, 1))
                 )
-                put(x, y0, new)
+                + (
+                    a[4] * jnp.where(z == 0, pltpu.roll(m, 1, 2), pltpu.roll(e, 1, 2))
+                    + a[5] * jnp.where(z == 127, pltpu.roll(m, 127, 2), pltpu.roll(e, 127, 2))
+                )
+            )
+            E[s + 1, rows] = new.reshape(64, 128)
+        EYS[s + 1, 0] = E2[pl.ds((s + 1) * 256, 16, stride=16), :]
+        EYS[s + 1, 1] = E2[pl.ds((s + 1) * 256 + 15, 16, stride=16), :]
+
+    def exchange(s):
+        ss, rs = sws.at[s], swr.at[s]
+        lo, hi = {"gy": lax.max(j - 1, 0)}, {"gy": lax.min(j + 1, 3)}
+        x_d = [
+            rdma(D.at[s, 1, inner], D.at[s, 17, inner], ss.at[2], rs.at[2], {"gx": i_lo}),
+            rdma(D.at[s, 16, inner], D.at[s, 0, inner], ss.at[3], rs.at[3], {"gx": i_hi}),
+        ]
+        x_e = [
+            rdma(E.at[s, pl.ds(0, 16)], EX.at[s, 1], ss.at[4], rs.at[4], {"gx": i_lo}),
+            rdma(E.at[s, pl.ds(240, 16)], EX.at[s, 0], ss.at[5], rs.at[5], {"gx": i_hi}),
+        ]
+        down_d = rdma(D.at[s, inner, 1], D.at[s, inner, 17], ss.at[0], rs.at[0], lo)
+        up_d = rdma(D.at[s, inner, 16], D.at[s, inner, 0], ss.at[1], rs.at[1], hi)
+        down_e = rdma(EYS.at[s, 0], EY.at[s, 1], ss.at[6], rs.at[6], lo)
+        up_e = rdma(EYS.at[s, 1], EY.at[s, 0], ss.at[7], rs.at[7], hi)
+        return x_d, x_e, down_d, up_d, down_e, up_e
+
+    faces(0)
+    for c in (ex_lo, ex_hi):
+        c.wait_recv()
+
+    def step(s, _):
+        x_d, x_e, down_d, up_d, down_e, up_e = exchange(s + 1)
+
+        def y_planes(x, _):
+            for y in (0, 15):
+                D[s + 1, x + 1, pl.ds(y + 1, 1)] = columns(s, x, y, 1)
             return 0
 
-        lax.fori_loop(0, 16, body, 0)
-
-    D2 = D.reshape(4 * 18 * 18 * 8, 128)
-
-    def base_of(s):
-        return (s * 18 * 18 + 19) * 8
-
-    def fix_ends(s, ref, base, width):
-        for half in range(2):
-            a, b = face_rows(D2, D2, half, base_of(s), 18)
-            fix = spread(
-                end_coef[half][0] * (ZR[s, 0, half][7:8] - b[7:8]),
-                end_coef[half][1] * (ZR[s, 1, half][0:1] - a[0:1]),
-            )
-            lo = jnp.where(lane128 < 64, fix, 0.0)
-            hi = fix - lo
-            for xx in range(8):
-                row = base + (half * 8 + xx) * width * 8
-                at = pl.ds(row, 16, stride=8)
-                ref[at, :] = ref[at, :] + lo[xx * 16 : xx * 16 + 16]
-                at = pl.ds(row + 7, 16, stride=8)
-                ref[at, :] = ref[at, :] + hi[xx * 16 : xx * 16 + 16]
-
-    def exchange(s):
-        out = [
-            rdma(ZSD.at[s, 0], ZR.at[s, 1], sws.at[s, 0], swr.at[s, 0], {"grp": l_lo}),
-            rdma(ZSD.at[s, 1], ZR.at[s, 0], sws.at[s, 1], swr.at[s, 1], {"grp": l_hi}),
-            rdma(D.at[s, 1, inner], D.at[s, 17, inner], sws.at[s, 2], swr.at[s, 2], {"gx": i_lo}),
-            rdma(D.at[s, 16, inner], D.at[s, 0, inner], sws.at[s, 3], swr.at[s, 3], {"gx": i_hi}),
-        ]
-        down = rdma(
-            D.at[s, inner, 1],
-            D.at[s, inner, 17],
-            sws.at[s, 4],
-            swr.at[s, 4],
-            {"gy": lax.max(j - 1, 0)},
-        )
-        up = rdma(
-            D.at[s, inner, 16],
-            D.at[s, inner, 0],
-            sws.at[s, 5],
-            swr.at[s, 5],
-            {"gy": lax.min(j + 1, 3)},
-        )
-        return out, down, up
-
-    def step(s, _):
-        def put(x, y0, new):
-            D[s + 1, x + 1, pl.ds(y0 + 1, 8)] = new
-
-        sweep(s, put)
-        fix_ends(s, D2, base_of(s + 1), 18)
-        for half in range(2):
-            a, b = face_rows(D2, D2, half, base_of(s + 1), 18)
-            ZSD[s + 1, 0, half] = a
-            ZSD[s + 1, 1, half] = b
-        out, down, up = exchange(s + 1)
-        for c in out:
-            c.start()
+        lax.fori_loop(0, 16, y_planes, 0)
 
         @pl.when(j > 0)
         def _():
-            down.start()
+            down_d.start()
 
         @pl.when(j < NGY - 1)
         def _():
-            up.start()
-
-        for c in out:
-            c.wait()
+            up_d.start()
+
+        for x in (0, 15):
+            for y0 in (1, 8):
+                D[s + 1, x + 1, pl.ds(y0 + 1, 7)] = columns(s, x, y0, 7)
+        for c in x_d:
+            c.start()
+
+        @pl.when(s == 0)
+        def _():
+            for c in ends_s:
+                c.wait_recv()
+            for part in range(4):
+                for n in range(7):
+                    at = part * 32 + (n * 4 if n < 6 else 0)
+                    up, down = (RA[1], RA[0]) if n < 6 else (RB[1], RB[0])
+                    AE[n, pl.ds(part * 64, 64)] = jnp.where(
+                        lane64 < 4,
+                        pltpu.roll(up, (128 - at) % 128, 1) if at else up,
+                        jnp.where(lane64 >= 124, pltpu.roll(down, 124 - at, 1), 0.0),
+                    )
+
+        beyond(s)
+        for c in x_e:
+            c.start()
 
         @pl.when(j > 0)
         def _():
-            down.wait_send()
-            up.wait_recv()
+            down_e.start()
 
         @pl.when(j < NGY - 1)
         def _():
-            up.wait_send()
-            down.wait_recv()
-
+            up_e.start()
+
+        def inside(x, _):
+            for y0 in (1, 8):
+                D[s + 1, x + 1, pl.ds(y0 + 1, 7)] = columns(s, x, y0, 7)
+            return 0
+
+        lax.fori_loop(1, 15, inside, 0)
+        faces(s + 1)
+
+        @pl.when(j > 0)
+        def _():
+            for c in (down_d, down_e):
+                c.wait_send()
+            for c in (up_d, up_e):
+                c.wait_recv()
+
+        @pl.when(j < NGY - 1)
+        def _():
+            for c in (up_d, up_e):
+                c.wait_send()
+            for c in (down_d, down_e):
+                c.wait_recv()
+
+        for c in x_d + x_e:
+            c.wait()
         return 0
 
     lax.fori_loop(0, 3, step, 0)
 
-    def put_last(x, y0, new):
-        OUT[x, y0 // 8] = PP[x + 1, pl.ds(y0 + 1, 8)] + new
-
-    sweep(3, put_last)
-    OUT2 = OUT.reshape(2048, 128)
-    fix_ends(3, OUT2, 0, 16)
+    def last_sweep(x, _):
+        for yt in range(2):
+            OUT[x, yt] = columns(3, x, yt * 8, 8)
+        return 0
+
+    lax.fori_loop(0, 16, last_sweep, 0)
 
     def store(ys, _):
         pltpu.make_async_copy(OUT.at[:, :, ys], out_hbm.at[:, :, :, ys, :], lsem.at[0]).start()
@@ -684,7 +809,7 @@
 
     lax.fori_loop(0, 8, store, 0)
 
-    for c in sends + xs + [zc_lo, zc_hi, vx_lo, vx_hi]:
+    for c in sends + xs + ends_s + [zc_lo, zc_hi, vx_lo, vx_hi, ex_lo, ex_hi]:
         c.wait_send()
 
     @pl.when(j > 0)
@@ -761,14 +886,25 @@
             vm(8, 8, 128),
             vm(256, 128),
             vm(256, 128),
-            vm(2, 2, 2, 8, 128),
-            vm(2, 2, 2, 8, 128),
-            vm(4, 2, 2, 8, 128),
-            vm(4, 2, 2, 8, 128),
+            vm(2, 64, 128),
+            vm(2, 64, 128),
+            vm(2, 64, 128),
+            vm(2, 64, 128),
+            vm(2, 64, 128),
+            vm(2, 64, 128),
+            vm(7, 256, 128),
+            vm(4, 256, 128),
+            vm(4, 2, 16, 128),
+            vm(4, 2, 16, 128),
+            vm(4, 2, 16, 128),
+            vm(256, 128),
+            vm(256, 128),
+            vm(256, 128),
+            vm(16, 8, 128),
             vm(8, 16, 8, 128),
-            vm(6, 8, 128),
             vm(8, 128),
-            vm(3, 4, 6, 8, 128),
+            vm(8, 128),
+            vm(3, 4, 8, 128),
             vm(3, 4, 8, 128),
             vm(8, 128),
             vm(2, 8, 128),
@@ -785,8 +921,10 @@
             dma((3, 4)),
             dma((2,)),
             dma((2,)),
-            dma((4, 6)),
-            dma((4, 6)),
+            dma((4,)),
+            dma((4,)),
+            dma((4, 8)),
+            dma((4, 8)),
         ],
         compiler_params=pltpu.CompilerParams(
             collective_id=0, has_side_effects=True, vmem_limit_bytes=60 * 1024 * 1024
@@ -805,8 +943,8 @@
         well_storage.reshape(1, 8),
         well_bhp_old.reshape(1, 8),
     )
-    new = out.transpose(0, 1, 3, 2, 4).reshape(16, 16, 1024)
-    return new, bhp.reshape(1, 1, 1, 8)
+    delta = out.transpose(0, 1, 3, 2, 4).reshape(16, 16, 1024)
+    return pressure + delta, bhp.reshape(1, 1, 1, 8)
 
 
 def solution(mesh):

time: 71.2 us -> 62.9 us (0.88)
  the two profiles are of different devices: /device:TPU:32 before, /device:TPU:1 now
where the time goes in v2:
time: 62.9 us; the launch traced here: 62.8 us
  Pallas kernels  59.2 us (94%)
  other arithmetic  2.38 us (4%)
  between operations  0.67 us (1%)
    pallas_call x1, Pallas kernels, per_device(): pl.pallas_call(kernel, out_shape=(jax.ShapeDtypeStruct((16, 2, 8, 8, 128)...  59.2 us
    add x1, other arithmetic, per_device(): return (pressure + delta, bhp.reshape(1, 1, 1, 8))  2.38 us

profile of v2, /device:TPU:1, one launch (start us, length us, event | category | flops | bytes accessed | tf_op | source)
XLA Modules:
  0.0 62.8 jit_solution(11854666945045794933)
XLA Ops:
  0.6 0.0 copy-start
  0.6 59.2 %shard_map.122 = (f32[16,2,8,8,128]{4,3,2,1,0:T(8,128)}, f32[1,8]{1,0:T(1,128)}) custom-call(s32[1,128]{1,0:T(1,128)} %bitcast.29, f32[16,2,8,8,128]{4,3,2,1,0:T(8,128)} %bitcast.24, f32[16,2,8,8,128]{4,3,2,1,0:T(8,128)} %bitcast.26, f32[16,2,8,8,128]{4,3,2,1,0:T(8,128)} %bitcast.27, f32[3,16,2,8,8,128]{5,4,3,2,1,0:T(8,128)} %bitcast.25, s32[1,128]{1,0:T(1,128)} %bitcast.30, ...), custom_call_target="tpu_custom_call" | custom-call | tf_op jit(solution)/shard_map/pallas_call | solution.py:856
  59.9 0.0 copy-start.1
  59.9 0.0 copy-done
  59.9 2.4 %bitcast_add_fusion = f32[16,16,1024]{2,1,0:T(8,128)} fusion(f32[16,16,1024]{2,1,0:T(8,128)S(1)} %copy-done, f32[16,2,8,8,128]{4,3,2,1,0:T(8,128)} %get-tuple-element.4), kind=kLoop, calls=%fused_computation | loop fusion | flops 262144 | bytes 3145728 | tf_op jit(solution)/shard_map/add | solution.py:947
  62.3 0.0 copy-done.1
  62.3 0.5 copy.14
Async XLA Ops:
  0.6 59.3 %copy-start = (f32[16,16,1024]{2,1,0:T(8,128)S(1)}, f32[16,16,1024]{2,1,0:T(8,128)}, u32[]{:S(2)}) copy-start(f32[16,16,1024]{2,1,0:T(8,128)} %param.11) | copy-start | bytes 3145732
  59.9 2.4 %copy-start.1 = (f32[1,8]{1,0:T(1,128)S(1)}, f32[1,8]{1,0:T(1,128)}, u32[]{:S(2)}) copy-start(f32[1,8]{1,0:T(1,128)} %get-tuple-element.5) | copy-start | bytes 100

commit v3 on v2

--- a/solution.py
+++ b/solution.py
@@ -59,7 +59,7 @@
     rate_v,
     stor_v,
     old_v,
-    out_hbm,
+    out_ref,
     bhp_out,
     PG,
     PP,
@@ -77,7 +77,6 @@
     CC,
     BB,
     D,
-    OUT,
     OH,
     PR,
     OWN,
@@ -152,6 +151,15 @@
     load_g = pltpu.make_async_copy(p_hbm, PG, lsem.at[0])
     load_g.start()
 
+    def load_kz(ys, _):
+        for yt in range(2):
+            pltpu.make_async_copy(
+                k_hbm.at[2, :, yt, :, ys, :], KZ.at[:, yt * 8 + ys], lsem.at[4]
+            ).start()
+        return 0
+
+    lax.fori_loop(0, 8, load_kz, 0)
+
     def load(ys, _):
         for yt in range(2):
             y = yt * 8 + ys
@@ -164,7 +172,6 @@
             pltpu.make_async_copy(
                 k_hbm.at[1, :, yt, :, ys, :], KY.at[:, 1 + y], lsem.at[3]
             ).start()
-            pltpu.make_async_copy(k_hbm.at[2, :, yt, :, ys, :], KZ.at[:, y], lsem.at[4]).start()
             pltpu.make_async_copy(po_hbm.at[:, yt, :, ys, :], PO.at[:, y], lsem.at[5]).start()
             pltpu.make_async_copy(ac_hbm.at[:, yt, :, ys, :], AC.at[:, y], lsem.at[6]).start()
         return 0
@@ -209,30 +216,6 @@
     )
     W1[i] = share
 
-    pl.semaphore_wait(bar, 23)
-
-    sends = []
-    for d in range(1, NGX):
-        c = rdma(W1.at[i], W1.at[i], a1s.at[d], a1r.at[i], {"gx": lax.rem(i + d, NGX)})
-        c.start()
-        sends.append(c)
-
-    zplane = jnp.zeros((16, 8, 128), F32)
-
-    @pl.when(j == 0)
-    def _():
-        PP[pl.ds(1, 16), 0] = zplane
-        for s in range(1, 4):
-            D[s, pl.ds(1, 16), 0] = zplane
-            EY[s, 0] = jnp.zeros((16, 128), F32)
-
-    @pl.when(j == NGY - 1)
-    def _():
-        PP[pl.ds(1, 16), 17] = zplane
-        for s in range(1, 4):
-            D[s, pl.ds(1, 16), 17] = zplane
-            EY[s, 1] = jnp.zeros((16, 128), F32)
-
     lane64 = iota((64, 128), 1)
 
     def end_rows(ref, part, k, base, width):
@@ -244,31 +227,86 @@
             axis=0,
         )
 
+    def flat(ref):
+        ref2 = ref.reshape(2048, 128)
+        return (
+            lambda part: end_rows(ref2, part, 0, 0, 16),
+            lambda part: end_rows(ref2, part, 7, 0, 16),
+        )
+
+    def raw_rows(k):
+        def rows(part):
+            return jnp.concatenate(
+                [PG[part * 4 + u, yt, k] for u in range(4) for yt in range(2)], axis=0
+            )
+
+        return rows
+
+    def pack_tile(refs, lo_ref, hi_ref):
+        keep = 4 if len(refs) == 1 else 1
+        lo = hi = jnp.zeros((8, 128), F32)
+        for part in range(4):
+            for n, ends in enumerate(refs):
+                a, b = ends[0](part), ends[1](part)
+                for u in range(8):
+                    to = part * 32 + u * 4 + n
+                    at = slice(u * 8, u * 8 + 8)
+                    a8 = jnp.where(lane < keep, a[at], 0.0)
+                    b8 = jnp.where(lane >= 128 - keep, b[at], 0.0)
+                    lo = lo + (pltpu.roll(a8, to, 1) if to else a8)
+                    hi = hi + pltpu.roll(b8, (to + keep) % 128, 1)
+        lo_ref[...] = lo
+        hi_ref[...] = hi
+
     def pack_ends(refs, lo_ref, hi_ref):
         lo = hi = jnp.zeros((64, 128), F32)
         for part in range(4):
-            for n, (ref, base, width) in enumerate(refs):
+            for n, ends in enumerate(refs):
                 to = part * 32 + n * 4
-                a = jnp.where(lane64 < 4, end_rows(ref, part, 0, base, width), 0.0)
-                b = jnp.where(lane64 >= 124, end_rows(ref, part, 7, base, width), 0.0)
+                a = jnp.where(lane64 < 4, ends[0](part), 0.0)
+                b = jnp.where(lane64 >= 124, ends[1](part), 0.0)
                 lo = lo + (pltpu.roll(a, to, 1) if to else a)
                 hi = hi + pltpu.roll(b, to + 4, 1)
         lo_ref[...] = lo
         hi_ref[...] = hi
 
-    PP2 = PP.reshape(18 * 18 * 8, 128)
-    KZ2 = KZ.reshape(2048, 128)
-    for ref, hbm, sem in ((PP.at[pl.ds(1, 16), pl.ds(1, 16)], KZ, 1), (KZ, KZ, 4)):
-        pltpu.make_async_copy(KZ, ref, lsem.at[sem]).wait()
-    pack_ends(((PP2, 19 * 8, 18), (KZ2, 0, 16)), ZS0.at[0], ZS0.at[1])
-    pltpu.make_async_copy(KZ, KX.at[pl.ds(1, 16)], lsem.at[2]).wait()
-    pltpu.make_async_copy(KZ, KY.at[:, pl.ds(1, 16)], lsem.at[3]).wait()
-
-    inner = pl.ds(1, 16)
+    pltpu.make_async_copy(KZ, KZ, lsem.at[4]).wait()
+    pack_tile([(raw_rows(0), raw_rows(7)), flat(KZ)], ZS0.at[0], ZS0.at[1])
+
+
+    pl.semaphore_wait(bar, 23)
+
+    sends = []
+    for d in range(1, NGX):
+        c = rdma(W1.at[i], W1.at[i], a1s.at[d], a1r.at[i], {"gx": lax.rem(i + d, NGX)})
+        c.start()
+        sends.append(c)
+
     zc_lo = rdma(ZS0.at[0], ZI.at[1], ihs.at[0], ihr.at[0], {"grp": l_lo})
     zc_hi = rdma(ZS0.at[1], ZI.at[0], ihs.at[1], ihr.at[1], {"grp": l_hi})
     zc_lo.start()
     zc_hi.start()
+
+    zplane = jnp.zeros((16, 8, 128), F32)
+
+    @pl.when(j == 0)
+    def _():
+        PP[pl.ds(1, 16), 0] = zplane
+        for s in range(1, 4):
+            D[s, pl.ds(1, 16), 0] = zplane
+            EY[s, 0] = jnp.zeros((16, 128), F32)
+
+    @pl.when(j == NGY - 1)
+    def _():
+        PP[pl.ds(1, 16), 17] = zplane
+        for s in range(1, 4):
+            D[s, pl.ds(1, 16), 17] = zplane
+            EY[s, 1] = jnp.zeros((16, 128), F32)
+
+    inner = pl.ds(1, 16)
+    pltpu.make_async_copy(KZ, KX.at[pl.ds(1, 16)], lsem.at[2]).wait()
+    pltpu.make_async_copy(KZ, KY.at[:, pl.ds(1, 16)], lsem.at[3]).wait()
+    pltpu.make_async_copy(KZ, PP.at[pl.ds(1, 16), pl.ds(1, 16)], lsem.at[1]).wait()
     xs = [
         rdma(KX.at[1], KX.at[17], ihs.at[2], ihr.at[2], {"gx": i_lo}),
         rdma(KX.at[16], KX.at[0], ihs.at[3], ihr.at[3], {"gx": i_hi}),
@@ -362,15 +400,13 @@
 
     has_lo = (l > 0).astype(F32)
     has_hi = (l < NGRP - 1).astype(F32)
-    for part in range(4):
-        rows = pl.ds(part * 64, 64)
+    for g in range(32):
         for n, ref in enumerate((HZP, HZK)):
-            at = part * 32 + n * 4
-            lo = pltpu.roll(ZI[0], (128 - at - 3) % 128, 1)
-            hi = pltpu.roll(ZI[1], 127 - at, 1)
+            lo = pltpu.roll(ZI[0], (128 - g * 4 - n) % 128, 1) if g + n else ZI[0]
+            hi = pltpu.roll(ZI[1], 127 - g * 4 - n, 1)
             if n:
                 lo, hi = lo * has_lo, hi * has_hi
-            ref[rows] = jnp.where(lane64 == 0, lo, hi)
+            ref[pl.ds(g * 8, 8)] = jnp.where(lane == 0, lo, hi)
 
     sh3 = (8, 8, 128)
     first = (iota(sh3, 2) == 0) & (iota(sh3, 1) == 0)
@@ -483,8 +519,24 @@
     to_peers(CSO, CS, css, csr)
     CS[1, j] = CSO[...]
 
-    def flat(ref):
-        return (ref.reshape(2048, 128), 0, 16)
+    for d in range(1, NGRP):
+        s = lax.rem(l + d, NGRP)
+        rdma(W2.at[l], W2.at[s], a2s.at[d], a2r.at[s], {"grp": s}).wait_recv()
+    acc8 = W2[0]
+    for s in range(1, NGRP):
+        acc8 = acc8 + W2[s]
+    bhp = jnp.where(sub < 4, acc8 / jnp.where(sub < 4, pltpu.roll(acc8, 4, 0), 1.0), 0.0)
+    mine = pltpu.roll(jnp.where(sub == own_row, bhp, 0.0), lax.rem(128 - shift, 128), 1)
+    bhp_out[...] = jnp.sum(mine, axis=0, keepdims=True)[:, 0:8]
+    bhp_c = jnp.sum(
+        jnp.where(sub == q_hi, nn(bhp, pick), 0.0), axis=0, keepdims=True
+    )
+
+    cx, cy, ck = cb // 128, lax.rem(cb // 8, 16), lax.rem(cb, 8)
+    spot = (sub128 == (cx // 4) * 32 + (cy // 4) * 8 + ck).astype(F32)
+    CBO[...] = scale * (nt(total * bhp_c, spot) - r_c)
+    to_peers(CBO, CB, cbs, cbr)
+    CB[1, j] = CBO[...]
 
     ends_s = [
         rdma(SA.at[0], RA.at[1], ras.at[0], rar.at[0], {"grp": l_lo}),
@@ -501,25 +553,6 @@
             lane64 < 64, end_rows(AZL2, part, 0, 0, 16), end_rows(AZH2, part, 7, 0, 16)
         )
 
-    for d in range(1, NGRP):
-        s = lax.rem(l + d, NGRP)
-        rdma(W2.at[l], W2.at[s], a2s.at[d], a2r.at[s], {"grp": s}).wait_recv()
-    acc8 = W2[0]
-    for s in range(1, NGRP):
-        acc8 = acc8 + W2[s]
-    bhp = jnp.where(sub < 4, acc8 / jnp.where(sub < 4, pltpu.roll(acc8, 4, 0), 1.0), 0.0)
-    mine = pltpu.roll(jnp.where(sub == own_row, bhp, 0.0), lax.rem(128 - shift, 128), 1)
-    bhp_out[...] = jnp.sum(mine, axis=0, keepdims=True)[:, 0:8]
-    bhp_c = jnp.sum(
-        jnp.where(sub == q_hi, nn(bhp, pick), 0.0), axis=0, keepdims=True
-    )
-
-    cx, cy, ck = cb // 128, lax.rem(cb // 8, 16), lax.rem(cb, 8)
-    spot = (sub128 == (cx // 4) * 32 + (cy // 4) * 8 + ck).astype(F32)
-    CBO[...] = scale * (nt(total * bhp_c, spot) - r_c)
-    to_peers(CBO, CB, cbs, cbr)
-    CB[1, j] = CBO[...]
-
     bhp_col = jnp.sum(jnp.where(sub128 == lane128, bhp_c, 0.0), axis=1, keepdims=True)
     wb_parts = halves(wi * bhp_col)
 
@@ -528,7 +561,7 @@
         return 0
 
     lax.fori_loop(0, 16, finish, 0)
-    pack_ends([flat(BB)], SB.at[0], SB.at[1])
+    pack_tile([flat(BB)], SB.at[0], SB.at[1])
     ends_s[2].start()
     ends_s[3].start()
 
@@ -606,15 +639,6 @@
     ex_hi = rdma(E.at[0, pl.ds(240, 16)], EX.at[0, 0], sws.at[0, 5], swr.at[0, 5], {"gx": i_hi})
     ex_lo.start()
     ex_hi.start()
-    vx_lo.wait_recv()
-    vx_hi.wait_recv()
-    for n, big, at in ((0, 3, 0), (1, 0, 17)):
-        up = upright(VX[n])
-        for row in range(1, 5):
-            t = cell(up, big, row)
-            for y in range(row * 4 - 3, row * 4 + 1):
-                D[0, at, y] = t
-
     D2 = D.reshape(4 * 18 * 18 * 8, 128)
     E2 = E.reshape(4 * 256, 128)
 
@@ -631,27 +655,32 @@
                 lane64 < 64, pltpu.roll(d, 1, 1), pltpu.roll(d, 127, 1)
             )
 
-    def columns(s, x, y0, n):
-        at = pl.ds(y0, n)
-        v = D[s, x + 1, pl.ds(y0 + 1, n)]
+    def columns(s, x, y, n, along_x=False):
+        at = (pl.ds(x, n), y) if along_x else (x, pl.ds(y, n))
+
+        def near(dx, dy):
+            if along_x:
+                return D[s, pl.ds(x + 1 + dx, n), y + 1 + dy]
+            return D[s, x + 1 + dx, pl.ds(y + 1 + dy, n)]
+
+        v = near(0, 0)
         shape = (n, 8, 128)
         k, z = iota(shape, 1), iota(shape, 2)
         ends = ((k == 0) & (z == 0)) | ((k == 7) & (z == 127))
         fix = jnp.concatenate(
             [
-                jnp.broadcast_to(FR[pl.ds(x * 16 + y0 + u, 1), :], (8, 128))[None]
+                jnp.broadcast_to(
+                    FR[pl.ds(x * 16 + y + u * (16 if along_x else 1), 1), :], (8, 128)
+                )[None]
                 for u in range(n)
             ],
             axis=0,
         )
         return (
-            (KEEP * v + BB[x, at])
-            + (
-                AXL[x, at] * D[s, x, pl.ds(y0 + 1, n)]
-                + AXH[x, at] * D[s, x + 2, pl.ds(y0 + 1, n)]
-            )
-            + (AYL[x, at] * D[s, x + 1, at] + AYH[x, at] * D[s, x + 1, pl.ds(y0 + 2, n)])
-            + (AZL[x, at] * z_below(v) + AZH[x, at] * z_above(v))
+            (KEEP * v + BB[at])
+            + (AXL[at] * near(-1, 0) + AXH[at] * near(1, 0))
+            + (AYL[at] * near(0, -1) + AYH[at] * near(0, 1))
+            + (AZL[at] * z_below(v) + AZH[at] * z_above(v))
             + jnp.where(ends, fix, 0.0)
         )
 
@@ -714,19 +743,59 @@
         up_e = rdma(EYS.at[s, 1], EY.at[s, 0], ss.at[7], rs.at[7], hi)
         return x_d, x_e, down_d, up_d, down_e, up_e
 
+    def put_d(s):
+        def put(x, y, new, along_x=False):
+            n = new.shape[0]
+            if along_x:
+                D[s, pl.ds(x + 1, n), y + 1] = new
+            else:
+                D[s, x + 1, pl.ds(y + 1, n)] = new
+
+        return put
+
+    def put_out(x, y, new, along_x=False):
+        for u in range(new.shape[0]):
+            xu, yu = (x + u, y) if along_x else (x, y + u)
+            row = xu * 128 + yu // 8 * 64 + yu % 8
+            out_ref[pl.ds(row, 8, stride=8), :] = new[u]
+
+    def inside(s, put):
+        def body(x, _):
+            for y in (1, 8):
+                put(x, y, columns(s, x, y, 7))
+            return 0
+
+        lax.fori_loop(1, 15, body, 0)
+
+    def y_planes(s, put):
+        def body(g, _):
+            for y in (0, 15):
+                put(g * 4, y, columns(s, g * 4, y, 4, True), True)
+            return 0
+
+        lax.fori_loop(0, 4, body, 0)
+
+    def x_planes(s, put):
+        for x in (0, 15):
+            for y in (1, 8):
+                put(x, y, columns(s, x, y, 7))
+
     faces(0)
+    inside(0, put_d(1))
     for c in (ex_lo, ex_hi):
         c.wait_recv()
-
-    def step(s, _):
+    vx_lo.wait_recv()
+    vx_hi.wait_recv()
+    for n, big, at in ((0, 3, 0), (1, 0, 17)):
+        up = upright(VX[n])
+        for row in range(1, 5):
+            t = cell(up, big, row)
+            for y in range(row * 4 - 3, row * 4 + 1):
+                D[0, at, y] = t
+
+    def step(s, put):
         x_d, x_e, down_d, up_d, down_e, up_e = exchange(s + 1)
-
-        def y_planes(x, _):
-            for y in (0, 15):
-                D[s + 1, x + 1, pl.ds(y + 1, 1)] = columns(s, x, y, 1)
-            return 0
-
-        lax.fori_loop(0, 16, y_planes, 0)
+        y_planes(s, put_d(s + 1))
 
         @pl.when(j > 0)
         def _():
@@ -736,9 +805,7 @@
         def _():
             up_d.start()
 
-        for x in (0, 15):
-            for y0 in (1, 8):
-                D[s + 1, x + 1, pl.ds(y0 + 1, 7)] = columns(s, x, y0, 7)
+        x_planes(s, put_d(s + 1))
         for c in x_d:
             c.start()
 
@@ -747,14 +814,19 @@
             for c in ends_s:
                 c.wait_recv()
             for part in range(4):
-                for n in range(7):
-                    at = part * 32 + (n * 4 if n < 6 else 0)
-                    up, down = (RA[1], RA[0]) if n < 6 else (RB[1], RB[0])
+                for n in range(6):
+                    at = part * 32 + n * 4
                     AE[n, pl.ds(part * 64, 64)] = jnp.where(
                         lane64 < 4,
-                        pltpu.roll(up, (128 - at) % 128, 1) if at else up,
-                        jnp.where(lane64 >= 124, pltpu.roll(down, 124 - at, 1), 0.0),
+                        pltpu.roll(RA[1], (128 - at) % 128, 1) if at else RA[1],
+                        jnp.where(lane64 >= 124, pltpu.roll(RA[0], 124 - at, 1), 0.0),
                     )
+            for g in range(32):
+                AE[6, pl.ds(g * 8, 8)] = jnp.where(
+                    lane < 4,
+                    pltpu.roll(RB[1], (128 - g * 4) % 128, 1) if g else RB[1],
+                    jnp.where(lane >= 124, pltpu.roll(RB[0], 124 - g * 4, 1) if g < 31 else RB[0], 0.0),
+                )
 
         beyond(s)
         for c in x_e:
@@ -768,13 +840,8 @@
         def _():
             up_e.start()
 
-        def inside(x, _):
-            for y0 in (1, 8):
-                D[s + 1, x + 1, pl.ds(y0 + 1, 7)] = columns(s, x, y0, 7)
-            return 0
-
-        lax.fori_loop(1, 15, inside, 0)
         faces(s + 1)
+        inside(s + 1, put)
 
         @pl.when(j > 0)
         def _():
@@ -792,22 +859,15 @@
 
         for c in x_d + x_e:
             c.wait()
+
+    def step_on(s, _):
+        step(s, put_d(s + 2))
         return 0
 
-    lax.fori_loop(0, 3, step, 0)
-
-    def last_sweep(x, _):
-        for yt in range(2):
-            OUT[x, yt] = columns(3, x, yt * 8, 8)
-        return 0
-
-    lax.fori_loop(0, 16, last_sweep, 0)
-
-    def store(ys, _):
-        pltpu.make_async_copy(OUT.at[:, :, ys], out_hbm.at[:, :, :, ys, :], lsem.at[0]).start()
-        return 0
-
-    lax.fori_loop(0, 8, store, 0)
+    lax.fori_loop(0, 2, step_on, 0)
+    step(2, put_out)
+    y_planes(3, put_out)
+    x_planes(3, put_out)
 
     for c in sends + xs + ends_s + [zc_lo, zc_hi, vx_lo, vx_hi, ex_lo, ex_hi]:
         c.wait_send()
@@ -821,8 +881,6 @@
     def _():
         for c in y_up:
             c.wait_send()
-
-    pltpu.make_async_copy(OUT, out_hbm, lsem.at[0]).wait()
 
 
 def tiles(a):
@@ -843,7 +901,7 @@
     well_bhp_old,
 ):
     perm = permeability.reshape(3, 16, 2, 8, 8, 128).transpose(0, 1, 2, 4, 3, 5)
-    hbm = pl.BlockSpec(memory_space=pl.ANY)
+    hbm = pl.BlockSpec(memory_space=pltpu.HBM)
     vmem = pl.BlockSpec(memory_space=pltpu.VMEM)
     smem = pl.BlockSpec(memory_space=pltpu.SMEM)
     grid = (16, 16, 8, 128)
@@ -856,11 +914,11 @@
     out, bhp = pl.pallas_call(
         kernel,
         out_shape=(
-            jax.ShapeDtypeStruct((16, 2, 8, 8, 128), F32),
+            jax.ShapeDtypeStruct((2048, 128), F32),
             jax.ShapeDtypeStruct((1, 8), F32),
         ),
         in_specs=[smem] + [hbm] * 4 + [vmem] * 7,
-        out_specs=(hbm, vmem),
+        out_specs=(vmem, vmem),
         scratch_shapes=[
             vm(16, 2, 8, 8, 128),
             vm(18, 18, 8, 128),
@@ -878,7 +936,6 @@
             vm(*grid),
             vm(*grid),
             vm(4, 18, 18, 8, 128),
-            vm(16, 2, 8, 8, 128),
             pltpu.VMEM((16, 128, 128), jnp.bfloat16),
             vm(128, 128),
             vm(8, 128),
@@ -886,12 +943,12 @@
             vm(8, 8, 128),
             vm(256, 128),
             vm(256, 128),
+            vm(2, 8, 128),
+            vm(2, 8, 128),
             vm(2, 64, 128),
             vm(2, 64, 128),
-            vm(2, 64, 128),
-            vm(2, 64, 128),
-            vm(2, 64, 128),
-            vm(2, 64, 128),
+            vm(2, 8, 128),
+            vm(2, 8, 128),
             vm(7, 256, 128),
             vm(4, 256, 128),
             vm(4, 2, 16, 128),
@@ -943,7 +1000,7 @@
         well_storage.reshape(1, 8),
         well_bhp_old.reshape(1, 8),
     )
-    delta = out.transpose(0, 1, 3, 2, 4).reshape(16, 16, 1024)
+    delta = out.reshape(16, 2, 8, 8, 128).transpose(0, 1, 3, 2, 4).reshape(16, 16, 1024)
     return pressure + delta, bhp.reshape(1, 1, 1, 8)
 
 

time: 62.9 us -> 54.7 us (0.87)
  Pallas kernels: 59.2 us -> 51 us
    pallas_call x1, Pallas kernels: 59.2 us -> 51 us  [per_device(): pl.pallas_call(kernel, out_shape=(jax.ShapeDtypeStruct((2048, 128), F32),...]
where the time goes in v3:
time: 54.7 us; the launch traced here: 54.6 us
  Pallas kernels  51 us (93%)
  other arithmetic  2.38 us (4%)
  between operations  0.67 us (1%)
    pallas_call x1, Pallas kernels, per_device(): pl.pallas_call(kernel, out_shape=(jax.ShapeDtypeStruct((2048, 128), F32),...  51 us
    add x1, other arithmetic, per_device(): return (pressure + delta, bhp.reshape(1, 1, 1, 8))  2.38 us

profile of v3, /device:TPU:1, one launch (start us, length us, event | category | flops | bytes accessed | tf_op | source)
XLA Modules:
  0.0 54.6 jit_solution(14837481891961510835)
XLA Ops:
  0.6 0.0 copy-start
  0.6 51.0 %shard_map.122 = (f32[2048,128]{1,0:T(8,128)}, f32[1,8]{1,0:T(1,128)}) custom-call(s32[1,128]{1,0:T(1,128)} %bitcast.31, f32[16,2,8,8,128]{4,3,2,1,0:T(8,128)} %bitcast.25, f32[16,2,8,8,128]{4,3,2,1,0:T(8,128)} %bitcast.28, f32[16,2,8,8,128]{4,3,2,1,0:T(8,128)} %bitcast.29, f32[3,16,2,8,8,128]{5,4,3,2,1,0:T(8,128)} %bitcast.26, s32[1,128]{1,0:T(1,128)} %bitcast.32, ...), custom_call_target="tpu_custom_call" | custom-call | tf_op jit(solution)/shard_map/pallas_call | solution.py:914
  51.6 0.0 copy-start.1
  51.7 0.0 copy-done
  51.7 2.4 %add.3 = f32[16,16,1024]{2,1,0:T(8,128)} add(f32[16,16,1024]{2,1,0:T(8,128)S(1)} %copy-done, f32[16,16,1024]{2,1,0:T(8,128)} %bitcast.27) | non-fusion elementwise | flops 262144 | bytes 3145728 | tf_op jit(solution)/shard_map/add | solution.py:1004
  54.0 0.0 copy-done.1
  54.0 0.5 copy.14
Async XLA Ops:
  0.6 51.0 %copy-start = (f32[16,16,1024]{2,1,0:T(8,128)S(1)}, f32[16,16,1024]{2,1,0:T(8,128)}, u32[]{:S(2)}) copy-start(f32[16,16,1024]{2,1,0:T(8,128)} %param.11) | copy-start | bytes 3145732
  51.6 2.4 %copy-start.1 = (f32[1,8]{1,0:T(1,128)S(1)}, f32[1,8]{1,0:T(1,128)}, u32[]{:S(2)}) copy-start(f32[1,8]{1,0:T(1,128)} %get-tuple-element.5) | copy-start | bytes 100

commit v4 on v3

--- a/solution.py
+++ b/solution.py
@@ -68,6 +68,10 @@
     KX,
     KY,
     KZ,
+    TX,
+    TY,
+    TZL,
+    TZH,
     AXL,
     AXH,
     AYL,
@@ -227,6 +231,8 @@
             axis=0,
         )
 
+    KZ2 = KZ.reshape(2048, 128)
+
     def flat(ref):
         ref2 = ref.reshape(2048, 128)
         return (
@@ -345,11 +351,48 @@
         lo = (v - hi.astype(F32)).astype(jnp.bfloat16)
         return jnp.concatenate([hi, lo], axis=1)
 
-    def blocks(x, parts):
-        r = jnp.dot(OH[x], parts, preferred_element_type=F32)
-        return (r[:, :128] + r[:, 128:]).reshape(16, 8, 128)
+    def blocks(x, n, parts):
+        rows = OH[pl.ds(x, n)].reshape(n * 128, 128)
+        r = jnp.dot(rows, parts, preferred_element_type=F32)
+        return (r[:, :128] + r[:, 128:]).reshape(n, 16, 8, 128)
 
     wi_parts = halves(wi)
+
+    CQ[...] = jnp.zeros((8, 16, 8, 128), F32)
+    pltpu.make_async_copy(KZ, PO, lsem.at[5]).wait()
+    pltpu.make_async_copy(KZ, AC, lsem.at[6]).wait()
+
+    def prepare(x, _):
+        w16 = blocks(x, 1, wi_parts)[0]
+        for yt in range(2):
+            y0 = yt * 8
+            c8 = pl.ds(y0, 8)
+            p = PP[x + 1, pl.ds(y0 + 1, 8)]
+            acc = AC[x, c8]
+            w = w16[y0 : y0 + 8]
+            PO[x, c8] = acc * (p - PO[x, c8]) + w * p
+            accw = acc + w
+            AC[x, c8] = accw
+            for yl in range(2):
+                CQ[1, x // 4 * 4 + yt * 2 + yl] += accw[yl * 4 : yl * 4 + 4].sum(0)
+            kz = KZ[x, c8]
+            tzl = harm(z_below(kz), kz)
+            TZL[x, c8] = tzl
+            TZH[x, c8] = z_above(tzl)
+            n = 8 - yt
+            lower, upper = KY[x, pl.ds(y0 + 1, n)], KY[x, pl.ds(y0 + 2, n)]
+            TY[x, pl.ds(y0 + 1, n)] = harm(lower, upper)
+        return 0
+
+    lax.fori_loop(0, 16, prepare, 0)
+
+    def faces_x(x, _):
+        for yt in range(2):
+            c8 = pl.ds(yt * 8, 8)
+            TX[x, c8] = harm(KX[x, c8], KX[x + 1, c8])
+        return 0
+
+    lax.fori_loop(1, 16, faces_x, 0)
 
     for d in range(1, NGX):
         s = lax.rem(i + d, NGX)
@@ -363,9 +406,6 @@
         c.start()
         sends.append(c)
 
-    CQ[...] = jnp.zeros((8, 16, 8, 128), F32)
-    pltpu.make_async_copy(KZ, PO, lsem.at[5]).wait()
-    pltpu.make_async_copy(KZ, AC, lsem.at[6]).wait()
     for c in xs:
         c.wait_recv()
 
@@ -379,9 +419,6 @@
         for c in y_down:
             c.wait_recv()
 
-    zc_lo.wait_recv()
-    zc_hi.wait_recv()
-
     @pl.when(i == 0)
     def _():
         KX[0] = zplane
@@ -398,6 +435,12 @@
     def _():
         KY[:, 17] = zplane
 
+    for x in (0, 16):
+        TX[x] = harm(KX[x], KX[x + 1])
+    for y in (0, 16):
+        TY[:, y] = harm(KY[:, y], KY[:, y + 1])
+    zc_lo.wait_recv()
+    zc_hi.wait_recv()
     has_lo = (l > 0).astype(F32)
     has_hi = (l < NGRP - 1).astype(F32)
     for g in range(32):
@@ -408,6 +451,12 @@
                 lo, hi = lo * has_lo, hi * has_hi
             ref[pl.ds(g * 8, 8)] = jnp.where(lane == 0, lo, hi)
 
+    for part in range(4):
+        rows = pl.ds(part * 64, 64)
+        k_end = jnp.where(
+            lane64 < 64, end_rows(KZ2, part, 0, 0, 16), end_rows(KZ2, part, 7, 0, 16)
+        )
+        HZK[rows] = harm(k_end, HZK[rows])
     sh3 = (8, 8, 128)
     first = (iota(sh3, 2) == 0) & (iota(sh3, 1) == 0)
     last = (iota(sh3, 2) == 127) & (iota(sh3, 1) == 7)
@@ -418,21 +467,17 @@
         )
 
     def operator(x, _):
-        w16 = blocks(x, wi_parts)
         big = x // 4
         f_lo = (lax.rem(x, 4) == 0).astype(F32)
         f_hi = (lax.rem(x, 4) == 3).astype(F32)
         for yt in range(2):
             y0 = yt * 8
             c8 = pl.ds(y0, 8)
-            kx = KX[x + 1, c8]
-            txl, txh = harm(KX[x, c8], kx), harm(kx, KX[x + 2, c8])
-            ky = KY[x, pl.ds(y0 + 1, 8)]
-            tyl, tyh = harm(KY[x, c8], ky), harm(ky, KY[x, pl.ds(y0 + 2, 8)])
-            kz = KZ[x, c8]
-            hk = column(HZK, x * 16 + y0)
-            tzl = harm(jnp.where(first, hk, z_below(kz)), kz)
-            tzh = harm(kz, jnp.where(last, hk, z_above(kz)))
+            txl, txh = TX[x, c8], TX[x + 1, c8]
+            tyl, tyh = TY[x, c8], TY[x, pl.ds(y0 + 1, 8)]
+            tk = column(HZK, x * 16 + y0)
+            tzl = jnp.where(first, tk, TZL[x, c8])
+            tzh = jnp.where(last, tk, TZH[x, c8])
             tsum = ((txl + txh) + (tyl + tyh)) + (tzl + tzh)
             p = PP[x + 1, pl.ds(y0 + 1, 8)]
             hp = column(HZP, x * 16 + y0)
@@ -444,11 +489,8 @@
                     + tzh * jnp.where(last, hp, z_above(p))
                 )
             )
-            acc = AC[x, c8]
-            w = w16[y0 : y0 + 8]
-            r0 = acc * (p - PO[x, c8]) + tsum * p - nb + w * p
-            accw = acc + w
-            c = RELAX * rcp(accw + tsum)
+            r0 = PO[x, c8] + tsum * p - nb
+            c = RELAX * rcp(AC[x, c8] + tsum)
             AXL[x, c8] = c * txl
             AXH[x, c8] = c * txh
             AYL[x, c8] = c * tyl
@@ -461,7 +503,6 @@
                 n = big * 4 + yt * 2 + yl
                 part = slice(yl * 4, yl * 4 + 4)
                 CQ[0, n] += r0[part].sum(0)
-                CQ[1, n] += accw[part].sum(0)
                 CQ[2, n] += txl[part].sum(0) * f_lo
                 CQ[3, n] += txh[part].sum(0) * f_hi
                 CQ[4, n] += tyl[yl * 4]
@@ -503,20 +544,24 @@
     )
     peers = [(dj, dz) for dj in range(NGY) for dz in range(3) if (dj, dz) != (0, 1)]
 
-    def to_peers(own_ref, all_ref, ss, rs):
+    def to_peers(own_ref, all_ref, ss, rs, count):
+        rows = pl.ds(0, count)
         for n, (dj, dz) in enumerate(peers):
             dev = {"gy": lax.rem(j + dj, NGY), "grp": lax.rem(l + dz + NGRP - 1, NGRP)}
-            c = rdma(own_ref, all_ref.at[2 - dz, j], ss.at[n], rs.at[2 - dz, j], dev)
+            to = all_ref.at[2 - dz, j, rows]
+            c = rdma(own_ref.at[rows], to, ss.at[n], rs.at[2 - dz, j], dev)
             c.start()
             sends.append(c)
 
-    def from_peers(own_ref, all_ref, ss, rs):
+    def from_peers(own_ref, all_ref, ss, rs, count):
+        rows = pl.ds(0, count)
         for n, (dj, dz) in enumerate(peers):
             s = lax.rem(j + dj, NGY)
             dev = {"gy": s, "grp": lax.rem(l + dz + NGRP - 1, NGRP)}
-            rdma(own_ref, all_ref.at[dz, s], ss.at[n], rs.at[dz, s], dev).wait_recv()
-
-    to_peers(CSO, CS, css, csr)
+            to = all_ref.at[dz, s, rows]
+            rdma(own_ref.at[rows], to, ss.at[n], rs.at[dz, s], dev).wait_recv()
+
+    to_peers(CSO, CS, css, csr, 8)
     CS[1, j] = CSO[...]
 
     for d in range(1, NGRP):
@@ -535,7 +580,7 @@
     cx, cy, ck = cb // 128, lax.rem(cb // 8, 16), lax.rem(cb, 8)
     spot = (sub128 == (cx // 4) * 32 + (cy // 4) * 8 + ck).astype(F32)
     CBO[...] = scale * (nt(total * bhp_c, spot) - r_c)
-    to_peers(CBO, CB, cbs, cbr)
+    to_peers(CBO, CB, cbs, cbr, 1)
     CB[1, j] = CBO[...]
 
     ends_s = [
@@ -556,33 +601,34 @@
     bhp_col = jnp.sum(jnp.where(sub128 == lane128, bhp_c, 0.0), axis=1, keepdims=True)
     wb_parts = halves(wi * bhp_col)
 
-    def finish(x, _):
-        BB[x] = BB[x] + CC[x] * blocks(x, wb_parts)
+    def finish(g, _):
+        at = pl.ds(g * 4, 4)
+        BB[at] = BB[at] + CC[at] * blocks(g * 4, 4, wb_parts)
         return 0
 
-    lax.fori_loop(0, 16, finish, 0)
+    lax.fori_loop(0, 4, finish, 0)
     pack_tile([flat(BB)], SB.at[0], SB.at[1])
     ends_s[2].start()
     ends_s[3].start()
 
-    def joined(all_ref):
+    def joined(tile):
         block = lax.rem(lane, 32) // 8
         for g in range(NGY):
             for y in range(4):
                 u = None
                 for dz in range(3):
-                    t = all_ref[dz, g]
+                    t = tile(dz, g)
                     to = (8 * (dz - y)) % 128
                     t = pltpu.roll(t, to, 1) if to else t
                     u = jnp.where(block == dz, t, 0.0 if u is None else u)
                 UU[g * 4 + y] = u
 
     UU2 = UU.reshape(128, 128)
-    from_peers(CSO, CS, css, csr)
-    joined(CS)
+    from_peers(CSO, CS, css, csr, 8)
+    joined(lambda dz, g: CS[dz, g])
     coef = [UU2[pl.ds(n, 16, stride=8), :] for n in range(6)]
-    from_peers(CBO, CB, cbs, cbr)
-    joined(CB)
+    from_peers(CBO, CB, cbs, cbr, 1)
+    joined(lambda dz, g: jnp.broadcast_to(CB[dz, g, 0:1], (8, 128)))
     rhs = UU2[pl.ds(0, 16, stride=8), :]
 
     def coarse_step(_, v):
@@ -726,22 +772,29 @@
         EYS[s + 1, 0] = E2[pl.ds((s + 1) * 256, 16, stride=16), :]
         EYS[s + 1, 1] = E2[pl.ds((s + 1) * 256 + 15, 16, stride=16), :]
 
-    def exchange(s):
+    gy_lo, gy_hi = {"gy": lax.max(j - 1, 0)}, {"gy": lax.min(j + 1, 3)}
+
+    def planes_of(s):
         ss, rs = sws.at[s], swr.at[s]
-        lo, hi = {"gy": lax.max(j - 1, 0)}, {"gy": lax.min(j + 1, 3)}
-        x_d = [
-            rdma(D.at[s, 1, inner], D.at[s, 17, inner], ss.at[2], rs.at[2], {"gx": i_lo}),
-            rdma(D.at[s, 16, inner], D.at[s, 0, inner], ss.at[3], rs.at[3], {"gx": i_hi}),
-        ]
-        x_e = [
-            rdma(E.at[s, pl.ds(0, 16)], EX.at[s, 1], ss.at[4], rs.at[4], {"gx": i_lo}),
-            rdma(E.at[s, pl.ds(240, 16)], EX.at[s, 0], ss.at[5], rs.at[5], {"gx": i_hi}),
-        ]
-        down_d = rdma(D.at[s, inner, 1], D.at[s, inner, 17], ss.at[0], rs.at[0], lo)
-        up_d = rdma(D.at[s, inner, 16], D.at[s, inner, 0], ss.at[1], rs.at[1], hi)
-        down_e = rdma(EYS.at[s, 0], EY.at[s, 1], ss.at[6], rs.at[6], lo)
-        up_e = rdma(EYS.at[s, 1], EY.at[s, 0], ss.at[7], rs.at[7], hi)
-        return x_d, x_e, down_d, up_d, down_e, up_e
+        return (
+            [
+                rdma(D.at[s, 1, inner], D.at[s, 17, inner], ss.at[2], rs.at[2], {"gx": i_lo}),
+                rdma(D.at[s, 16, inner], D.at[s, 0, inner], ss.at[3], rs.at[3], {"gx": i_hi}),
+            ],
+            rdma(D.at[s, inner, 1], D.at[s, inner, 17], ss.at[0], rs.at[0], gy_lo),
+            rdma(D.at[s, inner, 16], D.at[s, inner, 0], ss.at[1], rs.at[1], gy_hi),
+        )
+
+    def e_of(s):
+        ss, rs = sws.at[s], swr.at[s]
+        return (
+            [
+                rdma(E.at[s, pl.ds(0, 16)], EX.at[s, 1], ss.at[4], rs.at[4], {"gx": i_lo}),
+                rdma(E.at[s, pl.ds(240, 16)], EX.at[s, 0], ss.at[5], rs.at[5], {"gx": i_hi}),
+            ],
+            rdma(EYS.at[s, 0], EY.at[s, 1], ss.at[6], rs.at[6], gy_lo),
+            rdma(EYS.at[s, 1], EY.at[s, 0], ss.at[7], rs.at[7], gy_hi),
+        )
 
     def put_d(s):
         def put(x, y, new, along_x=False):
@@ -782,8 +835,6 @@
 
     faces(0)
     inside(0, put_d(1))
-    for c in (ex_lo, ex_hi):
-        c.wait_recv()
     vx_lo.wait_recv()
     vx_hi.wait_recv()
     for n, big, at in ((0, 3, 0), (1, 0, 17)):
@@ -793,8 +844,36 @@
             for y in range(row * 4 - 3, row * 4 + 1):
                 D[0, at, y] = t
 
-    def step(s, put):
-        x_d, x_e, down_d, up_d, down_e, up_e = exchange(s + 1)
+    def e_send(s):
+        x_e, down_e, up_e = e_of(s)
+        for c in x_e:
+            c.start()
+
+        @pl.when(j > 0)
+        def _():
+            down_e.start()
+
+        @pl.when(j < NGY - 1)
+        def _():
+            up_e.start()
+
+    def e_wait(s):
+        x_e, down_e, up_e = e_of(s)
+        for c in x_e:
+            c.wait()
+
+        @pl.when(j > 0)
+        def _():
+            down_e.wait_send()
+            up_e.wait_recv()
+
+        @pl.when(j < NGY - 1)
+        def _():
+            up_e.wait_send()
+            down_e.wait_recv()
+
+    def planes(s):
+        x_d, down_d, up_d = planes_of(s + 1)
         y_planes(s, put_d(s + 1))
 
         @pl.when(j > 0)
@@ -809,63 +888,62 @@
         for c in x_d:
             c.start()
 
-        @pl.when(s == 0)
-        def _():
-            for c in ends_s:
-                c.wait_recv()
-            for part in range(4):
-                for n in range(6):
-                    at = part * 32 + n * 4
-                    AE[n, pl.ds(part * 64, 64)] = jnp.where(
-                        lane64 < 4,
-                        pltpu.roll(RA[1], (128 - at) % 128, 1) if at else RA[1],
-                        jnp.where(lane64 >= 124, pltpu.roll(RA[0], 124 - at, 1), 0.0),
-                    )
-            for g in range(32):
-                AE[6, pl.ds(g * 8, 8)] = jnp.where(
-                    lane < 4,
-                    pltpu.roll(RB[1], (128 - g * 4) % 128, 1) if g else RB[1],
-                    jnp.where(lane >= 124, pltpu.roll(RB[0], 124 - g * 4, 1) if g < 31 else RB[0], 0.0),
-                )
-
-        beyond(s)
-        for c in x_e:
-            c.start()
+    def planes_wait(s):
+        x_d, down_d, up_d = planes_of(s + 1)
 
         @pl.when(j > 0)
         def _():
-            down_e.start()
+            down_d.wait_send()
+            up_d.wait_recv()
 
         @pl.when(j < NGY - 1)
         def _():
-            up_e.start()
-
-        faces(s + 1)
-        inside(s + 1, put)
-
-        @pl.when(j > 0)
-        def _():
-            for c in (down_d, down_e):
-                c.wait_send()
-            for c in (up_d, up_e):
-                c.wait_recv()
-
-        @pl.when(j < NGY - 1)
-        def _():
-            for c in (up_d, up_e):
-                c.wait_send()
-            for c in (down_d, down_e):
-                c.wait_recv()
-
-        for c in x_d + x_e:
+            up_d.wait_send()
+            down_d.wait_recv()
+
+        for c in x_d:
             c.wait()
 
-    def step_on(s, _):
-        step(s, put_d(s + 2))
-        return 0
-
-    lax.fori_loop(0, 2, step_on, 0)
-    step(2, put_out)
+    def ends_wait():
+        for c in ends_s:
+            c.wait_recv()
+        for part in range(4):
+            for n in range(6):
+                at = part * 32 + n * 4
+                AE[n, pl.ds(part * 64, 64)] = jnp.where(
+                    lane64 < 4,
+                    pltpu.roll(RA[1], (128 - at) % 128, 1) if at else RA[1],
+                    jnp.where(lane64 >= 124, pltpu.roll(RA[0], 124 - at, 1), 0.0),
+                )
+        for g in range(32):
+            up = pltpu.roll(RB[1], (128 - g * 4) % 128, 1) if g else RB[1]
+            down = pltpu.roll(RB[0], 124 - g * 4, 1) if g < 31 else RB[0]
+            AE[6, pl.ds(g * 8, 8)] = jnp.where(
+                lane < 4, up, jnp.where(lane >= 124, down, 0.0)
+            )
+
+    planes(0)
+    ends_wait()
+    for c in (ex_lo, ex_hi):
+        c.wait_recv()
+    beyond(0)
+    e_send(1)
+    faces(1)
+    inside(1, put_d(2))
+    planes_wait(0)
+    planes(1)
+    e_wait(1)
+    beyond(1)
+    e_send(2)
+    faces(2)
+    inside(2, put_d(3))
+    planes_wait(1)
+    planes(2)
+    e_wait(2)
+    beyond(2)
+    faces(3)
+    inside(3, put_out)
+    planes_wait(2)
     y_planes(3, put_out)
     x_planes(3, put_out)
 
@@ -926,6 +1004,10 @@
             vm(*grid),
             vm(18, 16, 8, 128),
             vm(16, 18, 8, 128),
+            vm(*grid),
+            vm(17, 16, 8, 128),
+            vm(16, 17, 8, 128),
+            vm(*grid),
             vm(*grid),
             vm(*grid),
             vm(*grid),

time: 54.7 us -> 50.9 us (0.931)
  Pallas kernels: 51 us -> 47.2 us
    pallas_call x1, Pallas kernels: 51 us -> 47.2 us  [per_device(): pl.pallas_call(kernel, out_shape=(jax.ShapeDtypeStruct((2048, 128), F32),...]
where the time goes in v4:
time: 50.9 us; the launch traced here: 50.8 us
  Pallas kernels  47.2 us (93%)
  other arithmetic  2.38 us (5%)
  between operations  0.67 us (1%)
  local copies, waits for them, and re-layouts  0.52 us (1%)
    pallas_call x1, Pallas kernels, per_device(): pl.pallas_call(kernel, out_shape=(jax.ShapeDtypeStruct((2048, 128), F32),...  47.2 us
    add x1, other arithmetic, per_device(): return (pressure + delta, bhp.reshape(1, 1, 1, 8))  2.38 us

profile of v4, /device:TPU:1, one launch (start us, length us, event | category | flops | bytes accessed | tf_op | source)
XLA Modules:
  0.0 50.8 jit_solution(15034448730406293201)
XLA Ops:
  0.6 0.0 copy-start
  0.6 47.2 %shard_map.122 = (f32[2048,128]{1,0:T(8,128)}, f32[1,8]{1,0:T(1,128)}) custom-call(s32[1,128]{1,0:T(1,128)} %bitcast.31, f32[16,2,8,8,128]{4,3,2,1,0:T(8,128)} %bitcast.25, f32[16,2,8,8,128]{4,3,2,1,0:T(8,128)} %bitcast.28, f32[16,2,8,8,128]{4,3,2,1,0:T(8,128)} %bitcast.29, f32[3,16,2,8,8,128]{5,4,3,2,1,0:T(8,128)} %bitcast.26, s32[1,128]{1,0:T(1,128)} %bitcast.32, ...), custom_call_target="tpu_custom_call" | custom-call | tf_op jit(solution)/shard_map/pallas_call | solution.py:992
  47.9 0.0 copy-start.1
  47.9 0.0 copy-done
  47.9 2.4 %add.3 = f32[16,16,1024]{2,1,0:T(8,128)} add(f32[16,16,1024]{2,1,0:T(8,128)S(1)} %copy-done, f32[16,16,1024]{2,1,0:T(8,128)} %bitcast.27) | non-fusion elementwise | flops 262144 | bytes 3145728 | tf_op jit(solution)/shard_map/add | solution.py:1086
  50.3 0.0 copy-done.1
  50.3 0.5 %copy.14 = f32[1,1,1,8]{3,2,1,0:T(1,128)} copy(f32[1,1,1,8]{3,2,1,0:T(1,128)S(1)} %bitcast.38) | data formatting | bytes 64
Async XLA Ops:
  0.6 47.3 %copy-start = (f32[16,16,1024]{2,1,0:T(8,128)S(1)}, f32[16,16,1024]{2,1,0:T(8,128)}, u32[]{:S(2)}) copy-start(f32[16,16,1024]{2,1,0:T(8,128)} %param.11) | copy-start | bytes 3145732
  47.9 2.4 %copy-start.1 = (f32[1,8]{1,0:T(1,128)S(1)}, f32[1,8]{1,0:T(1,128)}, u32[]{:S(2)}) copy-start(f32[1,8]{1,0:T(1,128)} %get-tuple-element.5) | copy-start | bytes 100

commit v5 on v4

--- a/solution.py
+++ b/solution.py
@@ -10,6 +10,7 @@
 RELAX = 0.7
 KEEP = 1.0 - RELAX
 NGX, NGY, NGRP = 8, 4, 8
+FAR_FIRST = (3, 5, 1, 7, 4, 2, 6)
 HIGH = lax.Precision.HIGHEST
 
 
@@ -23,8 +24,14 @@
     )
 
 
-def nn(a, b):
-    return jnp.dot(a, b, precision=HIGH, preferred_element_type=F32)
+def exact(a, onehot, dim):
+    hi = a.astype(jnp.bfloat16).astype(F32)
+    mid = (a - hi).astype(jnp.bfloat16).astype(F32)
+    parts = jnp.concatenate([hi, mid, a - hi - mid], axis=0).astype(jnp.bfloat16)
+    out = lax.dot_general(
+        parts, onehot, (((1,), (dim,)), ((), ())), preferred_element_type=F32
+    )
+    return (out[0:8] + out[8:16]) + out[16:24]
 
 
 def rcp(x):
@@ -47,11 +54,20 @@
 
 
 def kernel(
-    cb_s,
     p_hbm,
     po_hbm,
     ac_hbm,
     k_hbm,
+    cb_hbm,
+    ow_hbm,
+    cw_hbm,
+    wi_hbm,
+    rate_hbm,
+    stor_hbm,
+    old_hbm,
+    out_hbm,
+    bhp_hbm,
+    cb_s,
     cb_v,
     ow_v,
     cw_v,
@@ -59,7 +75,6 @@
     rate_v,
     stor_v,
     old_v,
-    out_ref,
     bhp_out,
     PG,
     PP,
@@ -81,6 +96,7 @@
     CC,
     BB,
     D,
+    OUT,
     OH,
     PR,
     OWN,
@@ -144,16 +160,33 @@
     def greet(dev):
         pl.semaphore_signal(bar, inc=1, device_id=dev, device_id_type=MESH)
 
+    for dz in (0, 2, 1):
+        for dj in range(1, NGY):
+            greet({"gy": lax.rem(j + dj, NGY), "grp": lax.rem(l + dz + NGRP - 1, NGRP)})
+    for d in FAR_FIRST:
+        greet({"grp": lax.rem(l + d, NGRP)})
     for d in range(1, NGX):
         greet({"gx": lax.rem(i + d, NGX)})
-    for d in range(1, NGRP):
-        greet({"grp": lax.rem(l + d, NGRP)})
-    for dj in range(1, NGY):
-        for dz in range(3):
-            greet({"gy": lax.rem(j + dj, NGY), "grp": lax.rem(l + dz + NGRP - 1, NGRP)})
 
     load_g = pltpu.make_async_copy(p_hbm, PG, lsem.at[0])
     load_g.start()
+    small = [
+        pltpu.make_async_copy(src, dst, lsem.at[7 + n])
+        for n, (src, dst) in enumerate(
+            (
+                (cb_hbm, cb_s),
+                (wi_hbm, wi_v),
+                (cb_hbm, cb_v),
+                (ow_hbm, ow_v),
+                (cw_hbm, cw_v),
+                (rate_hbm, rate_v),
+                (stor_hbm, stor_v),
+                (old_hbm, old_v),
+            )
+        )
+    ]
+    for c in small:
+        c.start()
 
     def load_kz(ys, _):
         for yt in range(2):
@@ -182,6 +215,8 @@
 
     lax.fori_loop(0, 8, load, 0)
 
+    for c in small:
+        c.wait()
     load_g.wait()
 
     def gather(g, _):
@@ -203,9 +238,9 @@
     cb = cb_v[...]
     q = ow_v[...] * 8 + cw_v[...]
     q_hi, q_lo = q // 128, lax.rem(q, 128)
-    pick = (sub128 == q_lo).astype(F32)
-    share = nt(
-        jnp.where(sub == q_hi, weighted, 0.0) + jnp.where(sub == q_hi + 4, total, 0.0), pick
+    pick = (sub128 == q_lo).astype(F32).astype(jnp.bfloat16)
+    share = exact(
+        jnp.where(sub == q_hi, weighted, 0.0) + jnp.where(sub == q_hi + 4, total, 0.0), pick, 1
     )
     own = i * NGRP + l
     own_row, shift = own // 16, lax.rem(own, 16) * 8
@@ -401,7 +436,7 @@
     for s in range(1, NGX):
         acc8 = acc8 + W1[s]
     W2[l] = acc8
-    for d in range(1, NGRP):
+    for d in FAR_FIRST:
         c = rdma(W2.at[l], W2.at[l], a2s.at[d], a2r.at[l], {"grp": lax.rem(l + d, NGRP)})
         c.start()
         sends.append(c)
@@ -542,7 +577,7 @@
         ],
         axis=0,
     )
-    peers = [(dj, dz) for dj in range(NGY) for dz in range(3) if (dj, dz) != (0, 1)]
+    peers = [(dj, dz) for dz in (0, 2, 1) for dj in range(NGY) if (dj, dz) != (0, 1)]
 
     def to_peers(own_ref, all_ref, ss, rs, count):
         rows = pl.ds(0, count)
@@ -563,6 +598,9 @@
 
     to_peers(CSO, CS, css, csr, 8)
     CS[1, j] = CSO[...]
+
+    cx, cy, ck = cb // 128, lax.rem(cb // 8, 16), lax.rem(cb, 8)
+    spot = (sub128 == (cx // 4) * 32 + (cy // 4) * 8 + ck).astype(F32).astype(jnp.bfloat16)
 
     for d in range(1, NGRP):
         s = lax.rem(l + d, NGRP)
@@ -573,13 +611,13 @@
     bhp = jnp.where(sub < 4, acc8 / jnp.where(sub < 4, pltpu.roll(acc8, 4, 0), 1.0), 0.0)
     mine = pltpu.roll(jnp.where(sub == own_row, bhp, 0.0), lax.rem(128 - shift, 128), 1)
     bhp_out[...] = jnp.sum(mine, axis=0, keepdims=True)[:, 0:8]
+    bhp_copy = pltpu.make_async_copy(bhp_out, bhp_hbm, lsem.at[15])
+    bhp_copy.start()
     bhp_c = jnp.sum(
-        jnp.where(sub == q_hi, nn(bhp, pick), 0.0), axis=0, keepdims=True
+        jnp.where(sub == q_hi, exact(bhp, pick, 0), 0.0), axis=0, keepdims=True
     )
 
-    cx, cy, ck = cb // 128, lax.rem(cb // 8, 16), lax.rem(cb, 8)
-    spot = (sub128 == (cx // 4) * 32 + (cy // 4) * 8 + ck).astype(F32)
-    CBO[...] = scale * (nt(total * bhp_c, spot) - r_c)
+    CBO[...] = scale * (exact(total * bhp_c, spot, 1) - r_c)
     to_peers(CBO, CB, cbs, cbr, 1)
     CB[1, j] = CBO[...]
 
@@ -649,17 +687,13 @@
     vx_lo.start()
     vx_hi.start()
 
-    def upright(tile):
-        return jnp.transpose(jnp.concatenate([tile] * 16, axis=0))
-
-    def cell(up, big, row):
-        t = jnp.where(lane == row, up[big * 32 + 8 : big * 32 + 16], 0.0)
+    def cell(tile, big, row):
+        t = jnp.where(lane == big * 32 + 8 + sub, tile[row : row + 1], 0.0)
         return jnp.broadcast_to(jnp.sum(t, axis=1, keepdims=True), (8, 128))
 
-    up = upright(mine)
     for big in range(4):
         for row in range(6):
-            t = cell(up, big, row)
+            t = cell(mine, big, row)
             ys = (0,) if row == 0 else (17,) if row == 5 else range(row * 4 - 3, row * 4 + 1)
             for x in range(4):
                 for y in ys:
@@ -806,11 +840,13 @@
 
         return put
 
+    OUT2 = OUT.reshape(2048, 128)
+
     def put_out(x, y, new, along_x=False):
         for u in range(new.shape[0]):
             xu, yu = (x + u, y) if along_x else (x, y + u)
             row = xu * 128 + yu // 8 * 64 + yu % 8
-            out_ref[pl.ds(row, 8, stride=8), :] = new[u]
+            OUT2[pl.ds(row, 8, stride=8), :] = new[u]
 
     def inside(s, put):
         def body(x, _):
@@ -838,9 +874,9 @@
     vx_lo.wait_recv()
     vx_hi.wait_recv()
     for n, big, at in ((0, 3, 0), (1, 0, 17)):
-        up = upright(VX[n])
+        tile = VX[n]
         for row in range(1, 5):
-            t = cell(up, big, row)
+            t = cell(tile, big, row)
             for y in range(row * 4 - 3, row * 4 + 1):
                 D[0, at, y] = t
 
@@ -943,10 +979,24 @@
     beyond(2)
     faces(3)
     inside(3, put_out)
+    some = pl.ds(1, 14)
+    first_out = pltpu.make_async_copy(OUT.at[some], out_hbm.at[some], lsem.at[0])
+    first_out.start()
     planes_wait(2)
+    first_out.wait()
     y_planes(3, put_out)
+    last_out = [
+        pltpu.make_async_copy(OUT.at[at], out_hbm.at[at], lsem.at[n])
+        for n, at in ((1, (some, 0, slice(None), 0)), (2, (some, 1, slice(None), 7)), (3, 0), (4, 15))
+    ]
+    for c in last_out[:2]:
+        c.start()
     x_planes(3, put_out)
-
+    for c in last_out[2:]:
+        c.start()
+
+    for c in last_out + [bhp_copy]:
+        c.wait()
     for c in sends + xs + ends_s + [zc_lo, zc_hi, vx_lo, vx_hi, ex_lo, ex_hi]:
         c.wait_send()
 
@@ -980,11 +1030,8 @@
 ):
     perm = permeability.reshape(3, 16, 2, 8, 8, 128).transpose(0, 1, 2, 4, 3, 5)
     hbm = pl.BlockSpec(memory_space=pltpu.HBM)
-    vmem = pl.BlockSpec(memory_space=pltpu.VMEM)
-    smem = pl.BlockSpec(memory_space=pltpu.SMEM)
     grid = (16, 16, 8, 128)
     dma = pltpu.SemaphoreType.DMA
-    cb = comp_block.reshape(1, 128)
 
     def vm(*shape):
         return pltpu.VMEM(shape, F32)
@@ -992,12 +1039,21 @@
     out, bhp = pl.pallas_call(
         kernel,
         out_shape=(
-            jax.ShapeDtypeStruct((2048, 128), F32),
+            jax.ShapeDtypeStruct((16, 2, 8, 8, 128), F32),
             jax.ShapeDtypeStruct((1, 8), F32),
         ),
-        in_specs=[smem] + [hbm] * 4 + [vmem] * 7,
-        out_specs=(vmem, vmem),
+        in_specs=[hbm] * 11,
+        out_specs=(hbm, hbm),
         scratch_shapes=[
+            pltpu.SMEM((1, 128), jnp.int32),
+            pltpu.VMEM((1, 128), jnp.int32),
+            pltpu.VMEM((1, 128), jnp.int32),
+            pltpu.VMEM((1, 128), jnp.int32),
+            vm(128, 128),
+            vm(1, 8),
+            vm(1, 8),
+            vm(1, 8),
+            vm(1, 8),
             vm(16, 2, 8, 8, 128),
             vm(18, 18, 8, 128),
             vm(*grid),
@@ -1018,6 +1074,7 @@
             vm(*grid),
             vm(*grid),
             vm(4, 18, 18, 8, 128),
+            vm(16, 2, 8, 8, 128),
             pltpu.VMEM((16, 128, 128), jnp.bfloat16),
             vm(128, 128),
             vm(8, 128),
@@ -1047,7 +1104,7 @@
             vm(3, 4, 8, 128),
             vm(8, 128),
             vm(2, 8, 128),
-            dma((7,)),
+            dma((16,)),
             dma((8,)),
             dma((8,)),
             dma((8,)),
@@ -1069,12 +1126,11 @@
             collective_id=0, has_side_effects=True, vmem_limit_bytes=60 * 1024 * 1024
         ),
     )(
-        cb,
         tiles(pressure),
         tiles(pressure_old),
         tiles(accumulation),
         perm,
-        cb,
+        comp_block.reshape(1, 128),
         comp_owner.reshape(1, 128),
         comp_well.reshape(1, 128),
         comp_wi.reshape(128, 128),
@@ -1082,7 +1138,7 @@
         well_storage.reshape(1, 8),
         well_bhp_old.reshape(1, 8),
     )
-    delta = out.reshape(16, 2, 8, 8, 128).transpose(0, 1, 3, 2, 4).reshape(16, 16, 1024)
+    delta = out.transpose(0, 1, 3, 2, 4).reshape(16, 16, 1024)
     return pressure + delta, bhp.reshape(1, 1, 1, 8)
 
 

time: 50.9 us -> 48.7 us (0.957)
  Pallas kernels: 47.2 us -> 44.8 us
    pallas_call x1, Pallas kernels: 47.2 us -> 44.8 us  [per_device(): pl.pallas_call(kernel, out_shape=(jax.ShapeDtypeStruct((16, 2, 8, 8, 128)...]
where the time goes in v5:
time: 48.7 us; the launch traced here: 48.3 us
  Pallas kernels  44.8 us (92%)
  other arithmetic  2.38 us (5%)
  between operations  0.67 us (1%)
  local copies, waits for them, and re-layouts  0.52 us (1%)
    pallas_call x1, Pallas kernels, per_device(): pl.pallas_call(kernel, out_shape=(jax.ShapeDtypeStruct((16, 2, 8, 8, 128)...  44.8 us
    add x1, other arithmetic, per_device(): return (pressure + delta, bhp.reshape(1, 1, 1, 8))  2.38 us

profile of v5, /device:TPU:1, one launch (start us, length us, event | category | flops | bytes accessed | tf_op | source)
XLA Modules:
  0.0 48.3 jit_solution(15483081343344863548)
XLA Ops:
  0.6 0.0 copy-start
  0.6 44.8 %shard_map.122 = (f32[16,2,8,8,128]{4,3,2,1,0:T(8,128)}, f32[1,8]{1,0:T(1,128)}) custom-call(f32[16,2,8,8,128]{4,3,2,1,0:T(8,128)} %bitcast.24, f32[16,2,8,8,128]{4,3,2,1,0:T(8,128)} %bitcast.26, f32[16,2,8,8,128]{4,3,2,1,0:T(8,128)} %bitcast.27, f32[3,16,2,8,8,128]{5,4,3,2,1,0:T(8,128)} %bitcast.25, s32[1,128]{1,0:T(1,128)} %bitcast.29, s32[1,128]{1,0:T(1,128)} %bitcast.30, ...), custom_call_target="tpu_custom_call" | custom-call | tf_op jit(solution)/shard_map/pallas_call | solution.py:1039
  45.4 0.0 copy-start.1
  45.4 0.0 copy-done
  45.4 2.4 %bitcast_add_fusion = f32[16,16,1024]{2,1,0:T(8,128)} fusion(f32[16,16,1024]{2,1,0:T(8,128)S(1)} %copy-done, f32[16,2,8,8,128]{4,3,2,1,0:T(8,128)} %get-tuple-element.4), kind=kLoop, calls=%fused_computation | loop fusion | flops 262144 | bytes 3145728 | tf_op jit(solution)/shard_map/add | solution.py:1142
  47.8 0.0 copy-done.1
  47.8 0.5 %copy.14 = f32[1,1,1,8]{3,2,1,0:T(1,128)} copy(f32[1,1,1,8]{3,2,1,0:T(1,128)S(1)} %bitcast.35) | data formatting | bytes 64
Async XLA Ops:
  0.6 44.8 %copy-start = (f32[16,16,1024]{2,1,0:T(8,128)S(1)}, f32[16,16,1024]{2,1,0:T(8,128)}, u32[]{:S(2)}) copy-start(f32[16,16,1024]{2,1,0:T(8,128)} %param.11) | copy-start | bytes 3145732
  45.4 2.4 %copy-start.1 = (f32[1,8]{1,0:T(1,128)S(1)}, f32[1,8]{1,0:T(1,128)}, u32[]{:S(2)}) copy-start(f32[1,8]{1,0:T(1,128)} %get-tuple-element.5) | copy-start | bytes 100

commit v6 on v5

--- a/solution.py
+++ b/solution.py
@@ -419,15 +419,7 @@
             TY[x, pl.ds(y0 + 1, n)] = harm(lower, upper)
         return 0
 
-    lax.fori_loop(0, 16, prepare, 0)
-
-    def faces_x(x, _):
-        for yt in range(2):
-            c8 = pl.ds(yt * 8, 8)
-            TX[x, c8] = harm(KX[x, c8], KX[x + 1, c8])
-        return 0
-
-    lax.fori_loop(1, 16, faces_x, 0)
+    lax.fori_loop(0, 3, prepare, 0)
 
     for d in range(1, NGX):
         s = lax.rem(i + d, NGX)
@@ -440,6 +432,16 @@
         c = rdma(W2.at[l], W2.at[l], a2s.at[d], a2r.at[l], {"grp": lax.rem(l + d, NGRP)})
         c.start()
         sends.append(c)
+
+    lax.fori_loop(3, 16, prepare, 0)
+
+    def faces_x(x, _):
+        for yt in range(2):
+            c8 = pl.ds(yt * 8, 8)
+            TX[x, c8] = harm(KX[x, c8], KX[x + 1, c8])
+        return 0
+
+    lax.fori_loop(1, 16, faces_x, 0)
 
     for c in xs:
         c.wait_recv()
@@ -609,17 +611,17 @@
     for s in range(1, NGRP):
         acc8 = acc8 + W2[s]
     bhp = jnp.where(sub < 4, acc8 / jnp.where(sub < 4, pltpu.roll(acc8, 4, 0), 1.0), 0.0)
+    bhp_c = jnp.sum(
+        jnp.where(sub == q_hi, exact(bhp, pick, 0), 0.0), axis=0, keepdims=True
+    )
+
+    CBO[...] = scale * (exact(total * bhp_c, spot, 1) - r_c)
+    to_peers(CBO, CB, cbs, cbr, 1)
+    CB[1, j] = CBO[...]
     mine = pltpu.roll(jnp.where(sub == own_row, bhp, 0.0), lax.rem(128 - shift, 128), 1)
     bhp_out[...] = jnp.sum(mine, axis=0, keepdims=True)[:, 0:8]
     bhp_copy = pltpu.make_async_copy(bhp_out, bhp_hbm, lsem.at[15])
     bhp_copy.start()
-    bhp_c = jnp.sum(
-        jnp.where(sub == q_hi, exact(bhp, pick, 0), 0.0), axis=0, keepdims=True
-    )
-
-    CBO[...] = scale * (exact(total * bhp_c, spot, 1) - r_c)
-    to_peers(CBO, CB, cbs, cbr, 1)
-    CB[1, j] = CBO[...]
 
     ends_s = [
         rdma(SA.at[0], RA.at[1], ras.at[0], rar.at[0], {"grp": l_lo}),
@@ -859,10 +861,10 @@
     def y_planes(s, put):
         def body(g, _):
             for y in (0, 15):
-                put(g * 4, y, columns(s, g * 4, y, 4, True), True)
+                put(g * 8, y, columns(s, g * 8, y, 8, True), True)
             return 0
 
-        lax.fori_loop(0, 4, body, 0)
+        lax.fori_loop(0, 2, body, 0)
 
     def x_planes(s, put):
         for x in (0, 15):

time: 48.7 us -> 47.1 us (0.967)
  Pallas kernels: 44.8 us -> 43.5 us
    pallas_call x1, Pallas kernels: 44.8 us -> 43.5 us  [per_device(): pl.pallas_call(kernel, out_shape=(jax.ShapeDtypeStruct((16, 2, 8, 8, 128)...]
where the time goes in v6:
time: 47.1 us; the launch traced here: 47 us
  Pallas kernels  43.5 us (92%)
  other arithmetic  2.38 us (5%)
  between operations  0.67 us (1%)
  local copies, waits for them, and re-layouts  0.52 us (1%)
    pallas_call x1, Pallas kernels, per_device(): pl.pallas_call(kernel, out_shape=(jax.ShapeDtypeStruct((16, 2, 8, 8, 128)...  43.5 us
    add x1, other arithmetic, per_device(): return (pressure + delta, bhp.reshape(1, 1, 1, 8))  2.38 us

profile of v6, /device:TPU:1, one launch (start us, length us, event | category | flops | bytes accessed | tf_op | source)
XLA Modules:
  0.0 47.0 jit_solution(11929974392114444222)
XLA Ops:
  0.6 0.0 copy-start
  0.6 43.5 %shard_map.122 = (f32[16,2,8,8,128]{4,3,2,1,0:T(8,128)}, f32[1,8]{1,0:T(1,128)}) custom-call(f32[16,2,8,8,128]{4,3,2,1,0:T(8,128)} %bitcast.24, f32[16,2,8,8,128]{4,3,2,1,0:T(8,128)} %bitcast.26, f32[16,2,8,8,128]{4,3,2,1,0:T(8,128)} %bitcast.27, f32[3,16,2,8,8,128]{5,4,3,2,1,0:T(8,128)} %bitcast.25, s32[1,128]{1,0:T(1,128)} %bitcast.29, s32[1,128]{1,0:T(1,128)} %bitcast.30, ...), custom_call_target="tpu_custom_call" | custom-call | tf_op jit(solution)/shard_map/pallas_call | solution.py:1041
  44.1 0.0 copy-start.1
  44.1 0.0 copy-done
  44.1 2.4 %bitcast_add_fusion = f32[16,16,1024]{2,1,0:T(8,128)} fusion(f32[16,16,1024]{2,1,0:T(8,128)S(1)} %copy-done, f32[16,2,8,8,128]{4,3,2,1,0:T(8,128)} %get-tuple-element.4), kind=kLoop, calls=%fused_computation | loop fusion | flops 262144 | bytes 3145728 | tf_op jit(solution)/shard_map/add | solution.py:1144
  46.5 0.0 copy-done.1
  46.5 0.5 %copy.14 = f32[1,1,1,8]{3,2,1,0:T(1,128)} copy(f32[1,1,1,8]{3,2,1,0:T(1,128)S(1)} %bitcast.35) | data formatting | bytes 64
Async XLA Ops:
  0.6 43.5 %copy-start = (f32[16,16,1024]{2,1,0:T(8,128)S(1)}, f32[16,16,1024]{2,1,0:T(8,128)}, u32[]{:S(2)}) copy-start(f32[16,16,1024]{2,1,0:T(8,128)} %param.11) | copy-start | bytes 3145732
  44.1 2.4 %copy-start.1 = (f32[1,8]{1,0:T(1,128)S(1)}, f32[1,8]{1,0:T(1,128)}, u32[]{:S(2)}) copy-start(f32[1,8]{1,0:T(1,128)} %get-tuple-element.5) | copy-start | bytes 100
